TPU v7x, 256 devices: a whole 4x4x8 slice. The times are simulated.
256 devices in a mesh: rep: 64 (over z, y, x_hi), fsdp: 4 (over x_lo, core).
Axes of the slice: x: 4 (x_hi: 2, x_lo: 2; x = x_hi * 2 + x_lo), y: 4, z: 8, core: 2. Of those that a mesh axis runs over, the one named last changes fastest.
Arguments:
- hidden_in: bfloat16 [65536, 8192], P(('rep', 'fsdp')), may hold values from -6 to 6
- norm_gain: float32 [8192], replicated, may hold values from 0.5 to 1.5
- key_weight: bfloat16 [64, 8192, 512], P('rep', 'fsdp'), may hold values from -0.0625 to 0.0625
- key_cot: bfloat16 [65536, 512], P(('rep', 'fsdp')), may hold values from -3 to 3
- global_base: float32 [6144, 128], P('fsdp'), may hold values from -2 to 2, as said below
- replica_params: bfloat16 [64, 6144, 128], P('rep', 'fsdp'), may hold values from -2.25 to 2.25, as said below
- outer_momentum: float32 [6144, 128], P('fsdp'), may hold values from -2 to 2
- scale_exponents: int32 [6144], P('fsdp'), may hold values from -6 to -2
- dither_seeds: int32 [64, 6144], P('rep', 'fsdp'), may hold values from 0 to 1048575
- fragment_index: int32 [1], replicated, may hold values from 0 to 32748
Outputs:
- keys: bfloat16 [65536, 512], P(('rep', 'fsdp'))
- weight_grad: bfloat16 [64, 8192, 512], P('rep', 'fsdp')
- input_grad: bfloat16 [65536, 8192], P(('rep', 'fsdp'))
- new_base: float32 [6144, 128], P('fsdp')
- new_momentum: float32 [6144, 128], P('fsdp')
Inputs may be any that keep to these rules, and one draw needn't show every extreme that they name: `global_base`: every entry's magnitude lies between 0.25 and 2, and it is a bfloat16 value. `replica_params`: each entry has the sign of the same entry of global_base and differs from it by at most 0.25.
All inputs are finite; a program needn't handle non-finite values.
Results may differ from a plain program's by a relative error of at most 0.0034.
The roundings to bfloat16 on the way count: a program that leaves them out, or rounds other values in their place, can miss the bound.
Values may be sent and summed in bfloat16 or wider, within the bound.
No kernel may reach another device: no remote copies, remote signals or barrier semaphores. Data moves between devices by JAX's collectives and lax.ppermute only.
A program may use at most 128 MiB of HBM per device.

v0:
```python
import jax
import jax.numpy as jnp
from jax import lax
from jax.sharding import PartitionSpec as P

eps_norm = 1e-05
momentum_keep = 0.9
outer_rate = 0.7


def level_table(exponents):
    powers = jnp.arange(-6, -1, dtype=jnp.int32)
    values = jnp.array([64.0, 32.0, 16.0, 8.0, 4.0], dtype=jnp.float32)
    match = exponents[:, None] == powers[None, :]
    return jnp.sum(jnp.where(match, values[None, :], jnp.float32(0.0)), axis=1)


def dither_levels(seeds, fragment, lanes):
    lane = jnp.arange(lanes, dtype=jnp.int32)
    first = (seeds[:, None] + 7919 * lane[None, :] + 4099 * fragment) % 32749
    second = (first * first + 3 * first + 17) % 32749
    return second % 16


def inner_weights(hidden_in, norm_gain, weight, key_cot):
    values = hidden_in.astype(jnp.float32)
    model_width = values.shape[1]
    inv_rms = lax.rsqrt(jnp.sum(values * values, axis=1, keepdims=True) / model_width + eps_norm)
    normed = (values * inv_rms * norm_gain).astype(jnp.bfloat16)
    piece = lax.all_gather(weight, "fsdp", axis=0, tiled=True)
    columns = normed
    key_total = jnp.dot(columns, piece, preferred_element_type=jnp.float32)
    back_piece = lax.dot_general(
        key_cot, piece, (((1,), (1,)), ((), ())), preferred_element_type=jnp.float32
    )
    key_total, dnormed = (key_total, back_piece)
    keys = key_total.astype(jnp.bfloat16)
    columns = normed
    weight_grad = lax.psum_scatter(
        lax.dot_general(
            columns, key_cot, (((0,), (0,)), ((), ())), preferred_element_type=jnp.float32
        ),
        "fsdp",
        scatter_dimension=0,
        tiled=True,
    ).astype(jnp.bfloat16)
    scaled = norm_gain * dnormed
    inner = jnp.sum(scaled * values, axis=1, keepdims=True) / model_width
    cubed = inv_rms * inv_rms * inv_rms
    input_grad = (inv_rms * scaled - values * cubed * inner).astype(jnp.bfloat16)
    return (keys, weight_grad, input_grad)


def outer_step(
    global_base, replica_params, outer_momentum, scale_exponents, dither_seeds, fragment_index
):
    rows_here = global_base.shape[0]
    lanes = global_base.shape[1]
    third = rows_here // 3
    replicas = lax.axis_size("rep")
    level = level_table(scale_exponents)[:, None]
    step_size = 1.0 / level
    delta = global_base - replica_params[0].astype(jnp.float32)
    offset = (
        dither_levels(dither_seeds[0], fragment_index[0], lanes).astype(jnp.float32) + 0.5
    ) / 16.0
    code = jnp.clip(jnp.floor(delta * level + offset), -8.0, 7.0).astype(jnp.int32)
    shifted = code + 8
    packed = shifted[:third] + 1024 * shifted[third : 2 * third] + 1048576 * shifted[2 * third :]
    total = lax.psum(packed, "rep")
    field_low = total % 1024
    field_mid = total // 1024 % 1024
    field_high = total // 1048576
    code_sum = jnp.concatenate([field_low, field_mid, field_high], axis=0) - 8 * replicas
    outer_grad = code_sum.astype(jnp.float32) * (step_size / replicas)
    new_momentum = momentum_keep * outer_momentum + outer_grad
    new_base = global_base - outer_rate * (outer_grad + momentum_keep * new_momentum)
    return (new_base, new_momentum)


def per_device(
    hidden_in,
    norm_gain,
    key_weight,
    key_cot,
    global_base,
    replica_params,
    outer_momentum,
    scale_exponents,
    dither_seeds,
    fragment_index,
):
    weight = key_weight[0]
    keys, weight_grad, input_grad = inner_weights(hidden_in, norm_gain, weight, key_cot)
    new_base, new_momentum = outer_step(
        global_base, replica_params, outer_momentum, scale_exponents, dither_seeds, fragment_index
    )
    return (keys, weight_grad[None, :, :], input_grad, new_base, new_momentum)


def solution(mesh):
    placed = (
        P(("rep", "fsdp"), None),
        P(),
        P("rep", "fsdp", None),
        P(("rep", "fsdp"), None),
        P("fsdp", None),
        P("rep", "fsdp", None),
        P("fsdp", None),
        P("fsdp"),
        P("rep", "fsdp"),
        P(),
    )
    return jax.shard_map(
        per_device,
        mesh=mesh,
        in_specs=placed,
        out_specs=(
            P(("rep", "fsdp"), None),
            P("rep", "fsdp", None),
            P(("rep", "fsdp"), None),
            P("fsdp", None),
            P("fsdp", None),
        ),
        check_vma=False,
    )
```

profile of v0, /device:TPU:130, one launch (start us, length us, event | category | flops | bytes accessed | tf_op | source)
XLA Modules:
  0.0 803.9 jit_solution(5407719856358158989)
XLA Ops:
  8.0 0.0 copy-start
  8.0 0.0 all-gather.3.cloned.1.call-start
  8.1 0.7 all-gather.3.cloned.1.call-update
  8.7 0.0 all-reduce.2.cloned.1.call-start
  9.4 0.7 reduce
  10.2 0.8 select_reduce_fusion
  11.0 3.4 fusion.26
  14.4 0.7 fusion.35
  15.1 0.0 all-reduce.2.cloned.1.call-update
  15.2 0.0 copy-start.5
  15.2 0.0 reduce-scatter.2.cloned.1.call-start
  15.2 79.8 %all-gather.3.cloned.1.call-done = bf16[1,8192,512]{2,1,0:T(8,128)(2,1)} async-done(((bf16[1,2048,512]{2,1,0:T(8,128)(2,1)}), bf16[1,8192,512]{2,1,0:T(8,128)(2,1)}) %all-gather.3.cloned.1.call-update) | async-done | bytes 8388624 | tf_op jit(solution)/shard_map/all_gather | solution.py:30
  95.0 0.0 copy-done
  95.0 0.0 copy-start.1
  95.0 12.0 %fusion.6 = (f32[256]{0:T(256)S(1)}, f32[256]{0:T(256)S(1)}, f32[256,8192]{1,0:T(8,128)}) fusion(bf16[256,8192]{1,0:T(8,128)(2,1)} %param.11, bf16[256,512]{1,0:T(8,128)(2,1)S(1)} %copy-done, bf16[1,8192,512]{2,1,0:T(8,128)(2,1)} %all-gather.3.cloned.1.call-done, f32[8192]{0:T(1024)} %param.12), kind=kOutput, calls=%fused_computation.11 | convolution fusion | flops 2160066048 | bytes 21268480 | tf_op jit(solution)/shard_map/dot_general | solution.py:33
  107.0 0.0 copy-done.5
  107.0 0.0 copy-done.1
  107.0 8.3 %fusion.13 = f32[8192,512]{1,0:T(8,128)} fusion(bf16[256,512]{1,0:T(8,128)(2,1)S(1)} %copy-done, bf16[256,8192]{1,0:T(8,128)(2,1)S(1)} %copy-done.1, f32[8192]{0:T(1024)S(1)} %copy-done.5, f32[256]{0:T(256)S(1)} %get-tuple-element.13), kind=kOutput, calls=%fused_computation.17 | convolution fusion | flops 2155872256 | bytes 21267456 | tf_op jit(solution)/shard_map/dot_general | solution.py:40
  115.3 0.0 copy-start.3
  115.3 0.0 reduce-scatter.2.cloned.1.call-update
  115.3 662.7 %all-reduce.2.cloned.1.call-done = s32[512,128]{1,0:T(8,128)} async-done(((s32[512,128]{1,0:T(8,128)}), s32[512,128]{1,0:T(8,128)}) %all-reduce.2.cloned.1.call-update) | async-done | bytes 262160 | tf_op jit(solution)/shard_map/psum | solution.py:70
  778.0 1.4 add_select_fusion.6
  779.4 0.0 copy-done.3
  779.4 0.0 copy-done.4
  779.4 0.0 slice-start
  779.4 1.5 multiply_subtract_fusion
  780.9 8.1 %fusion.10 = bf16[256,512]{1,0:T(8,128)(2,1)} fusion(bf16[1,8192,512]{2,1,0:T(8,128)(2,1)} %all-gather.3.cloned.1.call-done, bf16[256,8192]{1,0:T(8,128)(2,1)} %param.11, f32[8192]{0:T(1024)S(1)} %copy-done.5, f32[256]{0:T(256)S(1)} %get-tuple-element.13), kind=kOutput, calls=%fused_computation.16 | convolution fusion | flops 2156003328 | bytes 12878848 | tf_op jit(solution)/shard_map/dot_general | solution.py:32
  789.0 0.0 slice-done
  789.0 0.0 copy-done.2
  789.0 0.0 slice-done.1
  789.0 3.7 fusion.5
  792.6 3.8 convert_bitcast_fusion
  (10 shorter events, 0.0 us)
Async XLA Ops:
  8.0 87.0 %copy-start = (bf16[256,512]{1,0:T(8,128)(2,1)S(1)}, bf16[256,512]{1,0:T(8,128)(2,1)}, u32[]{:S(2)}) copy-start(bf16[256,512]{1,0:T(8,128)(2,1)} %param.14) | copy-start | bytes 786436
  8.0 87.0 %all-gather.3.cloned.1.call-start = ((), (), s32[]{:S(2)}) async-start(), calls=%async_computation.3 | async-start | bytes 10485760 | tf_op jit(solution)/shard_map/all_gather | solution.py:30
  8.7 769.3 %all-reduce.2.cloned.1.call-start = ((), (), s32[]{:S(2)}) async-start(), calls=%async_computation.2 | async-start | bytes 524288 | tf_op jit(solution)/shard_map/psum | solution.py:70
  15.2 91.9 %copy-start.5 = (f32[8192]{0:T(1024)S(1)}, f32[8192]{0:T(1024)}, u32[]{:S(2)}) copy-start(f32[8192]{0:T(1024)} %param.12) | copy-start | bytes 98308
  15.2 777.5 %reduce-scatter.2.cloned.1.call-start = ((), (), s32[]{:S(2)}) async-start(), calls=%async_computation.1 | async-start | bytes 20971520 | tf_op jit(solution)/shard_map/reduce_scatter | solution.py:39
  95.0 12.0 %copy-start.1 = (bf16[256,8192]{1,0:T(8,128)(2,1)S(1)}, bf16[256,8192]{1,0:T(8,128)(2,1)}, u32[]{:S(2)}) copy-start(bf16[256,8192]{1,0:T(8,128)(2,1)} %param.11) | copy-start | bytes 12582916
  115.3 664.1 %copy-start.3 = (f32[1536,128]{1,0:T(8,128)S(1)}, f32[1536,128]{1,0:T(8,128)}, u32[]{:S(2)}) copy-start(f32[1536,128]{1,0:T(8,128)} %param.15) | copy-start | bytes 2359300
  115.3 664.1 %copy-start.4 = (f32[1536,128]{1,0:T(8,128)S(1)}, f32[1536,128]{1,0:T(8,128)}, u32[]{:S(2)}) copy-start(f32[1536,128]{1,0:T(8,128)} %param.17) | copy-start | bytes 2359300
  779.4 9.6 %slice-start = ((s8[8388608]{0:T(1024)(128)(4,1)}), s8[4194304]{0:T(1024)(128)(4,1)S(1)}, s32[]{:S(2)}) async-start(s8[8388608]{0:T(1024)(128)(4,1)} %bitcast.17), calls=%async_computation.4 | async-start | bytes 8388608
  780.9 8.1 %copy-start.2 = (bf16[256,8192]{1,0:T(8,128)(2,1)S(1)}, bf16[256,8192]{1,0:T(8,128)(2,1)}, u32[]{:S(2)}) copy-start(bf16[256,8192]{1,0:T(8,128)(2,1)} %param.11) | copy-start | bytes 12582916
  780.9 8.1 %slice-start.1 = ((s8[8388608]{0:T(1024)(128)(4,1)}), s8[4194304]{0:T(1024)(128)(4,1)S(1)}, s32[]{:S(2)}) async-start(s8[8388608]{0:T(1024)(128)(4,1)} %bitcast.17), calls=%async_computation.5 | async-start | bytes 8388608
Sparse Core Ops, SparseCore 0:
  10.7 84.3 all-gather.2
  115.5 153.2 reduce-scatter.1
Sparse Core Ops, SparseCore 1:
  15.2 762.7 all-reduce.1
where the time goes:
time: 807 us; the launch traced here: 804 us
  waiting for transfers between devices  743 us (92%)
  matrix products  28.3 us (4%)
  between operations  16.2 us (2%)
  other arithmetic  16 us (2%)
    psum x1, waiting for transfers between devices, outer_step(): total = lax.psum(packed, 'rep')  663 us
    all_gather x1, waiting for transfers between devices, inner_weights(): piece = lax.all_gather(weight, 'fsdp', axis=0, tiled=True)  79.8 us
  transfers between devices with their start and end apart: 3, of which 2 were waited for; matrix products, arithmetic and copies ran while one was open for 5% of the time, Pallas kernels for 0%

commit v1 on v0

v1 whole, which is shorter than its diff:
```python
import functools

import jax
import jax.numpy as jnp
from jax import lax
from jax.experimental import pallas as pl
from jax.experimental.pallas import tpu as pltpu
from jax.sharding import PartitionSpec as P

eps_norm = 1e-05
momentum_keep = 0.9
outer_rate = 0.7
axes = ("rep", "fsdp")
f32 = jnp.float32
bf16 = jnp.bfloat16
cuts = (0, 1536, 2048)
small = pl.CostEstimate(flops=1024, bytes_accessed=1024, transcendentals=0)


def flip(bit):
    return [(i, i ^ bit) for i in range(256)]


core_bit, x_lo_bit, x_hi_bit, y_bit, z_bit = 1, 2, 4, 8, 32


def send(value, bit):
    return lax.ppermute(value, axes, flip(bit))


def params(limit=58):
    return pltpu.CompilerParams(vmem_limit_bytes=limit * 1024 * 1024)


def level_table(exponents):
    powers = jnp.arange(-6, -1, dtype=jnp.int32)
    values = jnp.array([64.0, 32.0, 16.0, 8.0, 4.0], dtype=jnp.float32)
    match = exponents[:, None] == powers[None, :]
    return jnp.sum(jnp.where(match, values[None, :], jnp.float32(0.0)), axis=1)


def dither_levels(seeds, fragment, lanes):
    lane = jnp.arange(lanes, dtype=jnp.int32)
    first = (seeds[:, None] + 7919 * lane[None, :] + 4099 * fragment) % 32749
    second = (first * first + 3 * first + 17) % 32749
    return second % 16


def norm_kernel(me_ref, x_ref, gain_ref, near_ref, f0_ref, f1_ref, f2_ref, f3_ref, inv_ref):
    width = x_ref.shape[1]
    slab = width // 4
    half = slab // 2
    total = jnp.zeros((x_ref.shape[0], 1), f32)
    for s in range(4):
        part = x_ref[:, s * slab : (s + 1) * slab].astype(f32)
        total = total + jnp.sum(part * part, axis=1, keepdims=True)
    inv = lax.rsqrt(total / width + eps_norm)
    inv_ref[...] = jnp.broadcast_to(inv, inv_ref.shape)
    me = me_ref[0]

    def normed(bits, offset, count):
        col = pl.multiple_of((me ^ bits) * slab + offset, half)
        part = x_ref[:, pl.ds(col, count)].astype(f32)
        return (part * inv * gain_ref[:, pl.ds(col, count)]).astype(bf16)

    near_ref[0] = normed(0, 0, slab)
    near_ref[1] = normed(2, 0, slab)
    f0_ref[...] = normed(1, 0, half)
    f1_ref[...] = normed(1, half, half)
    f2_ref[...] = normed(3, 0, half)
    f3_ref[...] = normed(3, half, half)


def norm_slabs(me, hidden, gain):
    rows, width = hidden.shape
    block = 64
    slab = width // 4
    near, *far, inv = pl.pallas_call(
        norm_kernel,
        grid_spec=pltpu.PrefetchScalarGridSpec(
            num_scalar_prefetch=1,
            grid=(rows // block,),
            in_specs=[
                pl.BlockSpec((block, width), lambda i, m: (i, 0)),
                pl.BlockSpec((1, width), lambda i, m: (0, 0)),
            ],
            out_specs=[pl.BlockSpec((2, block, slab), lambda i, m: (0, i, 0))]
            + [pl.BlockSpec((block, slab // 2), lambda i, m: (i, 0))] * 4
            + [pl.BlockSpec((block, 128), lambda i, m: (i, 0))],
        ),
        out_shape=[pltpu.HBM((2, rows, slab), bf16)]
        + [pltpu.HBM((rows, slab // 2), bf16)] * 4
        + [jax.ShapeDtypeStruct((rows, 128), f32)],
        compiler_params=params(),
        cost_estimate=small,
        name="norm",
    )(me, hidden, gain)
    return near, far, inv


def grad_kernel(mine_ref, low_ref, high_ref, cot_ref, cot_theirs_ref, *out_refs):
    over_tokens = (((0,), (0,)), ((), ()))
    step = 512
    half = low_ref.shape[1]
    for first, last, out_ref in zip(cuts, cuts[1:], out_refs):
        for row in range(first, last, step):
            theirs_ref = low_ref if row < half else high_ref
            a = mine_ref[0, :, row : row + step]
            b = theirs_ref[:, row % half : row % half + step]
            value = lax.dot_general(a, cot_ref[...], over_tokens, preferred_element_type=f32)
            value = value + lax.dot_general(b, cot_theirs_ref[...], over_tokens, preferred_element_type=f32)
            out_ref[row - first : row - first + step, :] = value.astype(out_ref.dtype)


def grad_rows(mine, theirs, cot, cot_theirs, place, dtype, name):
    _, tokens, slab = mine.shape
    width = cot.shape[1]
    counts = [b - a for a, b in zip(cuts, cuts[1:])]
    fixed = lambda i: (0, 0)
    return pl.pallas_call(
        grad_kernel,
        grid=(1,),
        in_specs=[
            pl.BlockSpec((1, tokens, slab), lambda i: (place, 0, 0)),
            pl.BlockSpec((tokens, slab // 2), fixed),
            pl.BlockSpec((tokens, slab // 2), fixed),
            pl.BlockSpec((tokens, width), fixed),
            pl.BlockSpec((tokens, width), fixed),
        ],
        out_specs=[pl.BlockSpec((rows, width), fixed) for rows in counts],
        out_shape=[pltpu.HBM((rows, width), dtype) for rows in counts],
        compiler_params=params(),
        cost_estimate=small,
        name=name,
    )(mine, theirs[2 * place], theirs[2 * place + 1], cot, cot_theirs)


def add_kernel(own_ref, came_ref, *refs):
    refs[-1][0] = (own_ref[...] + came_ref[...].astype(f32)).astype(bf16)


def add_rows(own, came, first, so_far):
    rows, width = own.shape
    block = 512
    part = pl.BlockSpec((block, width), lambda g: (g, 0))
    args = (own, came) if so_far is None else (own, came, so_far)
    return pl.pallas_call(
        add_kernel,
        grid=(rows // block,),
        in_specs=[part, part] + ([] if so_far is None else [pl.BlockSpec(memory_space=pl.ANY)]),
        out_specs=pl.BlockSpec((1, block, width), lambda g: (0, first // block + g, 0)),
        out_shape=jax.ShapeDtypeStruct((1, cuts[-1], width), bf16),
        input_output_aliases={} if so_far is None else {2: 0},
        compiler_params=params(),
        cost_estimate=small,
        name="add",
    )(*args)


def weight_specs(rows, block, width):
    specs = []
    first = 0
    for count in rows:
        steps = count // block

        def index(i, *_, first=first, steps=steps):
            return (jnp.clip(i - first, 0, steps - 1), 0)

        specs.append(pl.BlockSpec((block, width), index))
        first += steps
    return specs


def at_step(step, rows, block, refs, body):
    first = 0
    for count, ref in zip(rows, refs, strict=True):
        last = first + count // block

        @pl.when((step >= first) & (step < last))
        def _(ref=ref):
            body(ref)

        first = last


def keys_kernel(near_ref, *refs, rows, block, width):
    far = refs[:4]
    weights = refs[4 : 4 + len(rows)]
    cot_ref, inv_ref, keys_ref, factor_ref, total_ref = refs[4 + len(rows) :]
    step = pl.program_id(0)
    per = width // 4 // block

    @pl.when(step == 0)
    def _():
        total_ref[...] = jnp.zeros_like(total_ref)

    def near_body(w_ref):
        total_ref[...] += jnp.dot(near_ref[0], w_ref[...], preferred_element_type=f32)

    def far_body(w_ref):
        for k, part_ref in enumerate(far):

            @pl.when(step == per * (1 + 2 * (k // per)) + k % per)
            def _(part_ref=part_ref):
                total_ref[...] += jnp.dot(part_ref[...], w_ref[...], preferred_element_type=f32)

    is_near = (step // per) % 2 == 0

    @pl.when(is_near)
    def _():
        at_step(step, rows, block, weights, near_body)

    @pl.when(jnp.logical_not(is_near))
    def _():
        at_step(step, rows, block, weights, far_body)

    @pl.when(step == 4 * per - 1)
    def _():
        keys = total_ref[...]
        keys_ref[...] = keys.astype(bf16)
        dots = jnp.sum(cot_ref[...].astype(f32) * keys, axis=1, keepdims=True) / width
        inv = inv_ref[...]
        factor_ref[...] = inv * inv * dots


def keys_of(near, far, weights, cot, inv):
    _, tokens, slab = near.shape
    width = cot.shape[1]
    per = 2
    block = slab // per
    rows = [w.shape[0] for w in weights]

    def near_place(i):
        late = i >= 2 * per
        return (late.astype(jnp.int32), 0, jnp.minimum(jnp.where(late, i - 2 * per, i), per - 1))

    fixed = lambda i: (0, 0)
    return pl.pallas_call(
        functools.partial(keys_kernel, rows=rows, block=block, width=4 * slab),
        grid=(4 * per,),
        in_specs=[pl.BlockSpec((1, tokens, block), near_place)]
        + [pl.BlockSpec((tokens, block), fixed)] * 4
        + weight_specs(rows, block, width)
        + [pl.BlockSpec((tokens, width), fixed), pl.BlockSpec((tokens, 128), fixed)],
        out_specs=[pl.BlockSpec((tokens, width), fixed), pl.BlockSpec((tokens, 128), fixed)],
        out_shape=[jax.ShapeDtypeStruct((tokens, width), bf16), jax.ShapeDtypeStruct((tokens, 128), f32)],
        scratch_shapes=[pltpu.VMEM((tokens, width), f32)],
        compiler_params=params(),
        cost_estimate=small,
        name="keys",
    )(near, *far, *weights, cot, inv)


def input_kernel(me_ref, x_ref, gain_ref, *refs, rows, block):
    weights = refs[: len(rows)]
    cot_ref, inv_ref, factor_ref, out_ref = refs[len(rows) :]

    def body(w_ref):
        dnormed = lax.dot_general(
            cot_ref[...], w_ref[...], (((1,), (1,)), ((), ())), preferred_element_type=f32
        )
        scaled = gain_ref[...] * dnormed
        out_ref[...] = (inv_ref[:, :1] * scaled - x_ref[...].astype(f32) * factor_ref[:, :1]).astype(bf16)

    at_step(pl.program_id(0), rows, block, weights, body)


def input_grad_of(me, hidden, gain, weights, cot, inv, factor):
    tokens, total = hidden.shape
    width = cot.shape[1]
    per = 2
    block = total // 4 // per
    rows = [w.shape[0] for w in weights]

    def column(i, m):
        return (0, (m[0] ^ (i // per)) * per + i % per)

    fixed = lambda i, m: (0, 0)
    return pl.pallas_call(
        functools.partial(input_kernel, rows=rows, block=block),
        grid_spec=pltpu.PrefetchScalarGridSpec(
            num_scalar_prefetch=1,
            grid=(4 * per,),
            in_specs=[pl.BlockSpec((tokens, block), column), pl.BlockSpec((1, block), column)]
            + weight_specs(rows, block, width)
            + [
                pl.BlockSpec((tokens, width), fixed),
                pl.BlockSpec((tokens, 128), fixed),
                pl.BlockSpec((tokens, 128), fixed),
            ],
            out_specs=pl.BlockSpec((tokens, block), column),
        ),
        out_shape=jax.ShapeDtypeStruct((tokens, total), bf16),
        compiler_params=params(),
        cost_estimate=small,
        name="input_grad",
    )(me, hidden, gain, *weights, cot, inv, factor)


def packed_codes(global_base, replica_params, level, dither_seeds, fragment_index):
    rows_here, lanes = global_base.shape
    third = rows_here // 3
    delta = global_base - replica_params[0].astype(f32)
    offset = (dither_levels(dither_seeds[0], fragment_index[0], lanes).astype(f32) + 0.5) / 16.0
    code = jnp.clip(jnp.floor(delta * level + offset), -8.0, 7.0).astype(jnp.int32)
    shifted = code + 8
    return shifted[:third] + 1024 * shifted[third : 2 * third] + 1048576 * shifted[2 * third :]


def beside(got, work):
    return lax.optimization_barrier((got, work))


def halve(total, step, work):
    z = lax.axis_index("rep") // 8
    half = total.shape[0] // 2
    side = (z // step) % 2
    kept = lax.dynamic_slice_in_dim(total, side * half, half, 0)
    sent = lax.dynamic_slice_in_dim(total, (1 - side) * half, half, 0)
    got, done = beside(send(sent, z_bit * step), work())
    return kept + got, done


def exchange(total, masks, work):
    got, done = beside([send(total, mask) for mask in masks], work())
    return sum(got, total), done


def in_order(low, mine, other):
    return jnp.where(
        low, jnp.concatenate([mine, other], axis=0), jnp.concatenate([other, mine], axis=0)
    )


def rejoin_four(total, work):
    z = lax.axis_index("rep") // 8
    got, done = beside([send(total, z_bit * step) for step in (1, 2, 3)], work())
    even = z % 2 == 0
    near_pair = in_order(even, total, got[0])
    far_pair = in_order(even, got[1], got[2])
    return in_order((z // 2) % 2 == 0, near_pair, far_pair), done


def rejoin(total, step, work):
    z = lax.axis_index("rep") // 8
    other, done = beside(send(total, z_bit * step), work())
    return in_order((z // step) % 2 == 0, total, other), done


def outer_update(total, global_base, outer_momentum, level, replicas):
    step_size = 1.0 / level
    field_low = total & 1023
    field_mid = (total >> 10) & 1023
    field_high = total >> 20
    code_sum = jnp.concatenate([field_low, field_mid, field_high], axis=0) - 8 * replicas
    outer_grad = code_sum.astype(f32) * (step_size / replicas)
    new_momentum = momentum_keep * outer_momentum + outer_grad
    new_base = global_base - outer_rate * (outer_grad + momentum_keep * new_momentum)
    return (new_base, new_momentum)


def per_device(
    hidden_in,
    norm_gain,
    key_weight,
    key_cot,
    global_base,
    replica_params,
    outer_momentum,
    scale_exponents,
    dither_seeds,
    fragment_index,
):
    me = lax.axis_index("fsdp").astype(jnp.int32)[None]
    gain = norm_gain[None, :]
    own = key_weight[0]
    partner = send(own, x_lo_bit)
    sibling = send(own, core_bit)
    cot_sibling = send(key_cot, core_bit)
    nothing = lambda: ()

    level = level_table(scale_exponents)[:, None]
    total = packed_codes(global_base, replica_params, level, dither_seeds, fragment_index)
    total, hidden = lax.optimization_barrier((total, hidden_in))
    total, (near, far, inv) = halve(total, 4, lambda: norm_slabs(me, hidden, gain))
    total, came = halve(total, 2, lambda: [send(part, core_bit) for part in far])
    total, out_rows = exchange(
        total,
        (x_hi_bit | z_bit,),
        lambda: grad_rows(near, came, key_cot, cot_sibling, 1, bf16, "grad_out"),
    )
    in_rows = [send(rows, x_lo_bit) for rows in out_rows]
    total, _ = halve(total, 1, nothing)
    total, own_rows = exchange(
        total,
        (y_bit, y_bit * 2, y_bit * 3),
        lambda: grad_rows(near, came, key_cot, cot_sibling, 0, f32, "grad_own"),
    )
    total, partner = lax.optimization_barrier((total, partner))
    diagonal = send(partner, core_bit)
    total, diagonal = rejoin_four(total, lambda: diagonal)
    weights = (own, sibling, partner, diagonal)
    total, (keys, factor) = rejoin(total, 4, lambda: keys_of(near, far, weights, key_cot, inv))
    new_base, new_momentum = outer_update(
        total, global_base, outer_momentum, level, lax.axis_size("rep")
    )
    input_grad = input_grad_of(me, hidden, gain, weights, key_cot, inv, factor)
    input_grad, in_rows[0] = lax.optimization_barrier((input_grad, in_rows[0]))
    weight_grad = None
    for first, own_part, in_part in zip(cuts, own_rows, in_rows):
        weight_grad = add_rows(own_part, in_part, first, weight_grad)
    return (keys, weight_grad, input_grad, new_base, new_momentum)


def solution(mesh):
    placed = (
        P(("rep", "fsdp"), None),
        P(),
        P("rep", "fsdp", None),
        P(("rep", "fsdp"), None),
        P("fsdp", None),
        P("rep", "fsdp", None),
        P("fsdp", None),
        P("fsdp"),
        P("rep", "fsdp"),
        P(),
    )
    return jax.shard_map(
        per_device,
        mesh=mesh,
        in_specs=placed,
        out_specs=(
            P(("rep", "fsdp"), None),
            P("rep", "fsdp", None),
            P(("rep", "fsdp"), None),
            P("fsdp", None),
            P("fsdp", None),
        ),
        check_vma=False,
    )
```

time: 807 us -> 103 us (0.13)
  waiting for transfers between devices: 743 us -> 31 us
  Pallas kernels: 0 us -> 42.5 us
  matrix products: 28.3 us -> 0 us
  starting transfers between devices: 0.12 us -> 18 us
  between operations: 16.2 us -> 1.53 us
  other arithmetic: 16 us -> 6.56 us
    psum x1 -> x0, waiting for transfers between devices: 663 us -> none  [outer_step(): total = lax.psum(packed, 'rep')]
    all_gather x1 -> x0, waiting for transfers between devices: 79.8 us -> none  [inner_weights(): piece = lax.all_gather(weight, 'fsdp', axis=0, tiled=True)]
    pallas_call x0 -> x7, Pallas kernels: none -> 42.5 us  [the longest x1 11 us: input_grad_of(): pl.pallas_call(functools.partial(input_kernel, rows=rows, block=block), g...]
    ppermute x0 -> x21, waiting for transfers between devices: none -> 31 us  [send(): return lax.ppermute(value, axes, flip(bit))]
    dot_general x3 -> x0, matrix products: 28.3 us -> none  [the longest x1 12 us: inner_weights(): lax.dot_general(key_cot, piece, (((1,), (1,)), ((), ())), preferred_eleme...]
    ppermute x0 -> x21, starting transfers between devices: none -> 18 us  [send(): return lax.ppermute(value, axes, flip(bit))]
  transfers between devices with their start and end apart: 3 -> 21, of which waited for: 2 -> 10; matrix products, arithmetic and copies ran while one was open for 5% -> 7% of each run, Pallas kernels for 0% -> 40%
where the time goes in v1:
time: 103 us; the launch traced here: 101 us
  Pallas kernels  42.5 us (41%)
  waiting for transfers between devices  31 us (30%)
  starting transfers between devices  18 us (17%)
  other arithmetic  6.56 us (6%)
  local copies, waits for them, and re-layouts  1.56 us (2%)
  between operations  1.53 us (1%)
    ppermute x21, waiting for transfers between devices, send(): return lax.ppermute(value, axes, flip(bit))  31 us
    ppermute x21, starting transfers between devices, send(): return lax.ppermute(value, axes, flip(bit))  18 us
    pallas_call x1, Pallas kernels, input_grad_of(): pl.pallas_call(functools.partial(input_kernel, rows=rows, block=block), g...  11 us
    pallas_call x1, Pallas kernels, keys_of(): pl.pallas_call(functools.partial(keys_kernel, rows=rows, block=block, wid...  10.6 us
    pallas_call x2, Pallas kernels, grad_rows(): pl.pallas_call(grad_kernel, grid=(1,), in_specs=[pl.BlockSpec((1, tokens,...  8.69 us
    pallas_call x2, Pallas kernels, add_rows(): pl.pallas_call(add_kernel, grid=(rows // block,), in_specs=[part, part] +...  6.41 us
    pallas_call x1, Pallas kernels, norm_slabs(): pl.pallas_call(norm_kernel, grid_spec=pltpu.PrefetchScalarGridSpec(num_sc...  5.84 us
    add x1, other arithmetic, packed_codes(): shifted = code + 8  3.39 us
  transfers between devices with their start and end apart: 21, of which 10 were waited for; matrix products, arithmetic and copies ran while one was open for 7% of the time, Pallas kernels for 40%

profile of v1, /device:TPU:130, one launch (start us, length us, event | category | flops | bytes accessed | tf_op | source)
XLA Modules:
  0.0 101.1 jit_solution(12417792589413213319)
XLA Ops:
  0.6 0.6 collective-permute-start.12
  1.9 0.7 reduce
  2.6 0.8 select_reduce_fusion
  3.4 3.4 %fusion.10 = s32[1536,128]{1,0:T(8,128)S(1)} fusion(f32[1536,128]{1,0:T(8,128)} %param.15, bf16[1,1536,128]{2,1,0:T(8,128)(2,1)} %param.16, s32[]{:T(128)} %bitcast.1, s32[128]{0:T(128)S(1)} %iota_multiply_fusion, s32[1536]{0:T(1024)S(1)} %reduce, f32[1536]{0:T(1024)S(1)} %select_reduce_fusion), kind=kLoop, calls=%fused_computation.16 | loop fusion | flops 7667712 | bytes 1978884 | tf_op jit(solution)/shard_map/add | solution.py:306
  6.9 0.6 collective-permute-start
  7.5 5.8 %norm.1 = (bf16[2,256,2048]{2,1,0:T(8,128)(2,1)}, bf16[256,1024]{1,0:T(8,128)(2,1)}, bf16[256,1024]{1,0:T(8,128)(2,1)}, bf16[256,1024]{1,0:T(8,128)(2,1)}, bf16[...) custom-call(s32[1]{0:T(128)} %bitcast.2.me_ref, bf16[256,8192]{1,0:T(8,128)(2,1)} %x_ref.1, f32[1,8192]{1,0:T(1,128)} %bitcast.11), custom_call_target="tpu_custom_call" | custom-call | flops 1024 | bytes 1024 | tf_op jit(solution)/shard_map/norm/pallas_call | solution.py:78
  13.4 4.6 %collective-permute-done = s32[256,128]{1,0:T(8,128)S(1)} collective-permute-done((s32[256,128]{1,0:T(8,128)S(1)}, s32[256,128]{1,0:T(8,128)S(1)}, u32[]{:S(2)}, u32[]{:S(2)}) %collective-permute-start) | collective-permute-done | bytes 131104 | tf_op jit(solution)/shard_map/ppermute | solution.py:28
  18.0 2.2 %collective-permute-start.1 = (s32[128,128]{1,0:T(8,128)S(1)}, s32[128,128]{1,0:T(8,128)S(1)}, u32[]{:S(2)}, u32[]{:S(2)}) collective-permute-start(s32[128,128]{1,0:T(8,128)S(1)} %constant_dynamic-slice_fusion.1), channel_id=1, source_target_pairs={{0,64},{1,65},{2,66},{3,67},{4,68},{5,69},{6,70},{7,71},{8,72},{9,... | collective-permute-start | bytes 196616 | tf_op jit(solution)/shard_map/ppermute | solution.py:28
  20.7 2.6 %collective-permute-done.1 = s32[128,128]{1,0:T(8,128)S(1)} collective-permute-done((s32[128,128]{1,0:T(8,128)S(1)}, s32[128,128]{1,0:T(8,128)S(1)}, u32[]{:S(2)}, u32[]{:S(2)}) %collective-permute-start.1) | collective-permute-done | bytes 65568 | tf_op jit(solution)/shard_map/ppermute | solution.py:28
  23.3 0.6 collective-permute-start.7
  23.9 1.5 %collective-permute-done.5.high_ref = bf16[256,1024]{1,0:T(8,128)(2,1)S(1)} collective-permute-done((bf16[256,1024]{1,0:T(8,128)(2,1)}, bf16[256,1024]{1,0:T(8,128)(2,1)S(1)}, u32[]{:S(2)}, u32[]{:S(2)}) %collective-permute-start.5) | collective-permute-done | bytes 524320 | tf_op jit(solution)/shard_map/ppermute | solution.py:28
  25.4 3.6 %collective-permute-start.6 = (s32[128,128]{1,0:T(8,128)S(1)}, s32[128,128]{1,0:T(8,128)S(1)}, u32[]{:S(2)}, u32[]{:S(2)}) collective-permute-start(s32[128,128]{1,0:T(8,128)S(1)} %dynamic-slice_add_fusion.1), channel_id=1, source_target_pairs={{0,36},{1,37},{2,38},{3,39},{4,32},{5,33},{6,34},{7,35},{8,44},{9,... | collective-permute-start | bytes 196616 | tf_op jit(solution)/shard_map/ppermute | solution.py:28
  29.1 0.7 copy-done.3
  29.8 4.0 %grad_out.1 = (bf16[1536,512]{1,0:T(8,128)(2,1)}, bf16[512,512]{1,0:T(8,128)(2,1)}) custom-call(bf16[2,256,2048]{2,1,0:T(8,128)(2,1)} %get-tuple-element.64.mine_ref.near_ref, bf16[256,1024]{1,0:T(8,128)(2,1)} %copy-done.7, bf16[256,1024]{1,0:T(8,128)(2,1)} %copy-done.8, bf16[256,512]{1,0:T(8,128)(2,1)} %refs_4_.1, bf16[256,512]{1,0:T(8,128)(2,1)} %copy-done.3), custom_call_target="tpu_custom_call" | custom-call | flops 1024 | bytes 1024 | tf_op jit(solution)/shard_map/grad_out/pallas_call | solution.py:120
  34.3 3.6 %collective-permute-done.8 = s32[64,128]{1,0:T(8,128)S(1)} collective-permute-done((s32[64,128]{1,0:T(8,128)S(1)}, s32[64,128]{1,0:T(8,128)S(1)}, u32[]{:S(2)}, u32[]{:S(2)}) %collective-permute-start.8) | collective-permute-done | bytes 32800 | tf_op jit(solution)/shard_map/ppermute | solution.py:28
  37.9 3.1 %collective-permute-start.11 = (s32[64,128]{1,0:T(8,128)S(1)}, s32[64,128]{1,0:T(8,128)S(1)}, u32[]{:S(2)}, u32[]{:S(2)}) collective-permute-start(s32[64,128]{1,0:T(8,128)S(1)} %dynamic-slice_add_fusion.2), channel_id=1, source_target_pairs={{0,24},{1,25},{2,26},{3,27},{4,28},{5,29},{6,30},{7,31},{8,16},{9,... | collective-permute-start | bytes 98312 | tf_op jit(solution)/shard_map/ppermute | solution.py:28
  41.0 0.6 collective-permute-start.10
  42.1 4.7 %grad_own.1 = (f32[1536,512]{1,0:T(8,128)}, f32[512,512]{1,0:T(8,128)}) custom-call(bf16[2,256,2048]{2,1,0:T(8,128)(2,1)} %get-tuple-element.64.mine_ref.near_ref, bf16[256,1024]{1,0:T(8,128)(2,1)} %copy-done.5, bf16[256,1024]{1,0:T(8,128)(2,1)} %copy-done.6, bf16[256,512]{1,0:T(8,128)(2,1)} %refs_4_.1, bf16[256,512]{1,0:T(8,128)(2,1)} %copy-done.3), custom_call_target="tpu_custom_call" | custom-call | flops 1024 | bytes 1024 | tf_op jit(solution)/shard_map/grad_own/pallas_call | solution.py:120
  46.8 3.0 %collective-permute-done.12.refs_6_.refs_2_ = bf16[2048,512]{1,0:T(8,128)(2,1)} collective-permute-done((bf16[2048,512]{1,0:T(8,128)(2,1)}, bf16[2048,512]{1,0:T(8,128)(2,1)}, u32[]{:S(2)}, u32[]{:S(2)}) %collective-permute-start.12) | collective-permute-done | bytes 2097184 | tf_op jit(solution)/shard_map/ppermute | solution.py:28
  50.9 1.9 %collective-permute-start.15 = (s32[64,128]{1,0:T(8,128)S(1)}, s32[64,128]{1,0:T(8,128)S(1)}, u32[]{:S(2)}, u32[]{:S(2)}) collective-permute-start(s32[64,128]{1,0:T(8,128)S(1)} %add_add_fusion.1), channel_id=1, source_target_pairs={{0,96},{1,97},{2,98},{3,99},{4,100},{5,101},{6,102},{7,103},{8,104... | collective-permute-start | bytes 98312 | tf_op jit(solution)/shard_map/ppermute | solution.py:28
  53.3 3.2 %collective-permute-done.15 = s32[64,128]{1,0:T(8,128)S(1)} collective-permute-done((s32[64,128]{1,0:T(8,128)S(1)}, s32[64,128]{1,0:T(8,128)S(1)}, u32[]{:S(2)}, u32[]{:S(2)}) %collective-permute-start.15) | collective-permute-done | bytes 32800 | tf_op jit(solution)/shard_map/ppermute | solution.py:28
  56.6 1.0 collective-permute-done.14
  57.6 3.2 %collective-permute-done.13 = s32[64,128]{1,0:T(8,128)S(1)} collective-permute-done((s32[64,128]{1,0:T(8,128)S(1)}, s32[64,128]{1,0:T(8,128)S(1)}, u32[]{:S(2)}, u32[]{:S(2)}) %collective-permute-start.13) | collective-permute-done | bytes 32800 | tf_op jit(solution)/shard_map/ppermute | solution.py:28
  60.9 1.6 %collective-permute-start.19 = (bf16[512,512]{1,0:T(8,128)(2,1)S(1)}, bf16[512,512]{1,0:T(8,128)(2,1)S(1)}, u32[]{:S(2)}, u32[]{:S(2)}) collective-permute-start(bf16[512,512]{1,0:T(8,128)(2,1)S(1)} %copy-done.10), channel_id=1, source_target_pairs={{0,2},{1,3},{2,0},{3,1},{4,6},{5,7},{6,4},{7,5},{8,10},{9,11},{10,... | collective-permute-start | bytes 1572872 | tf_op jit(solution)/shard_map/ppermute | solution.py:28
  62.5 10.6 %keys.1 = (bf16[256,512]{1,0:T(8,128)(2,1)}, f32[256,128]{1,0:T(8,128)}) custom-call(bf16[2,256,2048]{2,1,0:T(8,128)(2,1)} %get-tuple-element.64.mine_ref.near_ref, bf16[256,1024]{1,0:T(8,128)(2,1)} %get-tuple-element.59.refs_0_, bf16[256,1024]{1,0:T(8,128)(2,1)} %get-tuple-element.60.refs_1_, bf16[256,1024]{1,0:T(8,128)(2,1)} %get-tuple-element.61.refs_2_, ...), custom_call_target="tpu_custom_call" | custom-call | flops 1024 | bytes 1024 | tf_op jit(solution)/shard_map/keys/pallas_call | solution.py:238
  73.1 11.0 %input_grad.1 = bf16[256,8192]{1,0:T(8,128)(2,1)} custom-call(s32[1]{0:T(128)} %bitcast.2.me_ref, bf16[256,8192]{1,0:T(8,128)(2,1)} %x_ref.1, f32[1,8192]{1,0:T(1,128)} %bitcast.12, bf16[2048,512]{1,0:T(8,128)(2,1)} %bitcast.9, bf16[2048,512]{1,0:T(8,128)(2,1)} %collective-permute-done.18.refs_5_.refs_1_, ...), custom_call_target="tpu_custom_call" | custom-call | flops 1024 | bytes 1024 | tf_op jit(solution)/shard_map/input_grad/pallas_call | solution.py:279
  84.1 3.8 %collective-permute-done.20.came_ref = bf16[1536,512]{1,0:T(8,128)(2,1)} collective-permute-done((bf16[1536,512]{1,0:T(8,128)(2,1)}, bf16[1536,512]{1,0:T(8,128)(2,1)}, u32[]{:S(2)}, u32[]{:S(2)}) %collective-permute-start.20) | collective-permute-done | bytes 1572896 | tf_op jit(solution)/shard_map/ppermute | solution.py:28
  87.9 4.2 %add.339.refs_0_ = bf16[1,2048,512]{2,1,0:T(8,128)(2,1)} custom-call(f32[1536,512]{1,0:T(8,128)} %get-tuple-element.89.own_ref, bf16[1536,512]{1,0:T(8,128)(2,1)} %collective-permute-done.20.came_ref), custom_call_target="tpu_custom_call" | custom-call | flops 1024 | bytes 1024 | tf_op jit(solution)/shard_map/add/pallas_call | solution.py:147
  92.2 1.5 %multiply_subtract_fusion = (f32[1536,128]{1,0:T(8,128)}, f32[1536,128]{1,0:T(8,128)}) fusion(f32[1536,128]{1,0:T(8,128)S(1)} %copy-done.2, s32[512,128]{1,0:T(8,128)S(1)} %get-tuple-element.99, s32[512,128]{1,0:T(8,128)S(1)} %get-tuple-element.98, s32[512,128]{1,0:T(8,128)S(1)} %get-tuple-element.97, f32[1536]{0:T(1024)S(1)} %divide_multiply_fusion, ...), kind=kLoop, calls=%fused_computation.22 | loop fusion | flops 2162688 | bytes 3938304 | tf_op jit(solution)/shard_map/sub | solution.py:358
  93.6 4.5 %collective-permute-done.19.came_ref = bf16[512,512]{1,0:T(8,128)(2,1)S(1)} collective-permute-done((bf16[512,512]{1,0:T(8,128)(2,1)S(1)}, bf16[512,512]{1,0:T(8,128)(2,1)S(1)}, u32[]{:S(2)}, u32[]{:S(2)}) %collective-permute-start.19) | collective-permute-done | bytes 524320 | tf_op jit(solution)/shard_map/ppermute | solution.py:28
  98.1 0.8 copy-done.9
  98.9 2.2 %add.340 = bf16[1,2048,512]{2,1,0:T(8,128)(2,1)} custom-call(f32[512,512]{1,0:T(8,128)} %get-tuple-element.87.own_ref, bf16[512,512]{1,0:T(8,128)(2,1)} %copy-done.9, bf16[1,2048,512]{2,1,0:T(8,128)(2,1)} %add.339.refs_0_), custom_call_target="tpu_custom_call", output_to_operand_aliasing={{}: (2, {})} | custom-call | flops 1024 | bytes 1024 | tf_op jit(solution)/shard_map/add/pallas_call | solution.py:147
  (58 shorter events, 3.4 us)
Async XLA Ops:
  0.6 49.2 %collective-permute-start.12 = (bf16[2048,512]{1,0:T(8,128)(2,1)}, bf16[2048,512]{1,0:T(8,128)(2,1)}, u32[]{:S(2)}, u32[]{:S(2)}) collective-permute-start(bf16[2048,512]{1,0:T(8,128)(2,1)} %bitcast.7), channel_id=1, source_target_pairs={{0,2},{1,3},{2,0},{3,1},{4,6},{5,7},{6,4},{7,5},{8,10},{9,11},{10,... | collective-permute-start | bytes 6291464 | tf_op jit(solution)/shard_map/ppermute | solution.py:28
  6.9 11.1 %collective-permute-start = (s32[256,128]{1,0:T(8,128)S(1)}, s32[256,128]{1,0:T(8,128)S(1)}, u32[]{:S(2)}, u32[]{:S(2)}) collective-permute-start(s32[256,128]{1,0:T(8,128)S(1)} %constant_dynamic-slice_fusion.2), channel_id=1, source_target_pairs={{0,128},{1,129},{2,130},{3,131},{4,132},{5,133},{6,134},{7,135},{8... | collective-permute-start | bytes 393224 | tf_op jit(solution)/shard_map/ppermute | solution.py:28
  7.5 15.8 %copy-start.1 = (bf16[256,512]{1,0:T(8,128)(2,1)S(1)}, bf16[256,512]{1,0:T(8,128)(2,1)}, u32[]{:S(2)}) copy-start(bf16[256,512]{1,0:T(8,128)(2,1)} %refs_4_.1) | copy-start | bytes 786436
  18.0 5.3 %collective-permute-start.1 = (s32[128,128]{1,0:T(8,128)S(1)}, s32[128,128]{1,0:T(8,128)S(1)}, u32[]{:S(2)}, u32[]{:S(2)}) collective-permute-start(s32[128,128]{1,0:T(8,128)S(1)} %constant_dynamic-slice_fusion.1), channel_id=1, source_target_pairs={{0,64},{1,65},{2,66},{3,67},{4,68},{5,69},{6,70},{7,71},{8,72},{9,... | collective-permute-start | bytes 196616 | tf_op jit(solution)/shard_map/ppermute | solution.py:28
  20.2 3.1 %collective-permute-start.2 = (bf16[256,1024]{1,0:T(8,128)(2,1)}, bf16[256,1024]{1,0:T(8,128)(2,1)S(1)}, u32[]{:S(2)}, u32[]{:S(2)}) collective-permute-start(bf16[256,1024]{1,0:T(8,128)(2,1)} %get-tuple-element.59.refs_0_), channel_id=1, source_target_pairs={{0,1},{1,0},{2,3},{3,2},{4,5},{5,4},{6,7},{7,6},{8,9},{9,8},{10,11... | collective-permute-start | bytes 1572872 | tf_op jit(solution)/shard_map/ppermute | solution.py:28
  20.2 3.7 %collective-permute-start.3 = (bf16[256,1024]{1,0:T(8,128)(2,1)}, bf16[256,1024]{1,0:T(8,128)(2,1)S(1)}, u32[]{:S(2)}, u32[]{:S(2)}) collective-permute-start(bf16[256,1024]{1,0:T(8,128)(2,1)} %get-tuple-element.60.refs_1_), channel_id=1, source_target_pairs={{0,1},{1,0},{2,3},{3,2},{4,5},{5,4},{6,7},{7,6},{8,9},{9,8},{10,11... | collective-permute-start | bytes 1572872 | tf_op jit(solution)/shard_map/ppermute | solution.py:28
  20.7 3.2 %collective-permute-start.4 = (bf16[256,1024]{1,0:T(8,128)(2,1)}, bf16[256,1024]{1,0:T(8,128)(2,1)S(1)}, u32[]{:S(2)}, u32[]{:S(2)}) collective-permute-start(bf16[256,1024]{1,0:T(8,128)(2,1)} %get-tuple-element.61.refs_2_), channel_id=1, source_target_pairs={{0,1},{1,0},{2,3},{3,2},{4,5},{5,4},{6,7},{7,6},{8,9},{9,8},{10,11... | collective-permute-start | bytes 1572872 | tf_op jit(solution)/shard_map/ppermute | solution.py:28
  23.3 2.1 %collective-permute-start.5 = (bf16[256,1024]{1,0:T(8,128)(2,1)}, bf16[256,1024]{1,0:T(8,128)(2,1)S(1)}, u32[]{:S(2)}, u32[]{:S(2)}) collective-permute-start(bf16[256,1024]{1,0:T(8,128)(2,1)} %get-tuple-element.62.refs_3_), channel_id=1, source_target_pairs={{0,1},{1,0},{2,3},{3,2},{4,5},{5,4},{6,7},{7,6},{8,9},{9,8},{10,11... | collective-permute-start | bytes 1572872 | tf_op jit(solution)/shard_map/ppermute | solution.py:28
  23.3 18.8 %copy-start.5 = (bf16[256,1024]{1,0:T(8,128)(2,1)}, bf16[256,1024]{1,0:T(8,128)(2,1)S(1)}, u32[]{:S(2)}) copy-start(bf16[256,1024]{1,0:T(8,128)(2,1)S(1)} %collective-permute-done.2.low_ref) | copy-start | bytes 1572868
  23.3 5.8 %collective-permute-start.7 = (bf16[256,512]{1,0:T(8,128)(2,1)S(1)}, bf16[256,512]{1,0:T(8,128)(2,1)S(1)}, u32[]{:S(2)}, u32[]{:S(2)}) collective-permute-start(bf16[256,512]{1,0:T(8,128)(2,1)S(1)} %copy-done.1), channel_id=1, source_target_pairs={{0,1},{1,0},{2,3},{3,2},{4,5},{5,4},{6,7},{7,6},{8,9},{9,8},{10,11... | collective-permute-start | bytes 786440 | tf_op jit(solution)/shard_map/ppermute | solution.py:28
  23.9 9.9 %copy-start.6 = (bf16[256,1024]{1,0:T(8,128)(2,1)}, bf16[256,1024]{1,0:T(8,128)(2,1)S(1)}, u32[]{:S(2)}) copy-start(bf16[256,1024]{1,0:T(8,128)(2,1)S(1)} %collective-permute-done.3.high_ref) | copy-start | bytes 1572868
  23.9 5.2 %copy-start.7 = (bf16[256,1024]{1,0:T(8,128)(2,1)}, bf16[256,1024]{1,0:T(8,128)(2,1)S(1)}, u32[]{:S(2)}) copy-start(bf16[256,1024]{1,0:T(8,128)(2,1)S(1)} %collective-permute-done.4.low_ref) | copy-start | bytes 1572868
  25.4 3.7 %copy-start.8 = (bf16[256,1024]{1,0:T(8,128)(2,1)}, bf16[256,1024]{1,0:T(8,128)(2,1)S(1)}, u32[]{:S(2)}) copy-start(bf16[256,1024]{1,0:T(8,128)(2,1)S(1)} %collective-permute-done.5.high_ref) | copy-start | bytes 1572868
  25.4 8.4 %collective-permute-start.6 = (s32[128,128]{1,0:T(8,128)S(1)}, s32[128,128]{1,0:T(8,128)S(1)}, u32[]{:S(2)}, u32[]{:S(2)}) collective-permute-start(s32[128,128]{1,0:T(8,128)S(1)} %dynamic-slice_add_fusion.1), channel_id=1, source_target_pairs={{0,36},{1,37},{2,38},{3,39},{4,32},{5,33},{6,34},{7,35},{8,44},{9,... | collective-permute-start | bytes 196616 | tf_op jit(solution)/shard_map/ppermute | solution.py:28
  29.1 0.7 copy-start.3
  33.8 16.0 %copy-start = (bf16[1,2048,512]{2,1,0:T(8,128)(2,1)S(1)}, bf16[1,2048,512]{2,1,0:T(8,128)(2,1)}, u32[]{:S(2)}) copy-start(bf16[1,2048,512]{2,1,0:T(8,128)(2,1)} %param.13) | copy-start | bytes 6291460
  33.9 4.0 %collective-permute-start.8 = (s32[64,128]{1,0:T(8,128)S(1)}, s32[64,128]{1,0:T(8,128)S(1)}, u32[]{:S(2)}, u32[]{:S(2)}) collective-permute-start(s32[64,128]{1,0:T(8,128)S(1)} %constant_dynamic-slice_fusion), channel_id=1, source_target_pairs={{0,32},{1,33},{2,34},{3,35},{4,36},{5,37},{6,38},{7,39},{8,40},{9,... | collective-permute-start | bytes 98312 | tf_op jit(solution)/shard_map/ppermute | solution.py:28
  37.9 23.1 %copy-start.10 = (bf16[512,512]{1,0:T(8,128)(2,1)S(1)}, bf16[512,512]{1,0:T(8,128)(2,1)}, u32[]{:S(2)}) copy-start(bf16[512,512]{1,0:T(8,128)(2,1)} %get-tuple-element.88) | copy-start | bytes 1572868
  37.9 8.9 %collective-permute-start.11 = (s32[64,128]{1,0:T(8,128)S(1)}, s32[64,128]{1,0:T(8,128)S(1)}, u32[]{:S(2)}, u32[]{:S(2)}) collective-permute-start(s32[64,128]{1,0:T(8,128)S(1)} %dynamic-slice_add_fusion.2), channel_id=1, source_target_pairs={{0,24},{1,25},{2,26},{3,27},{4,28},{5,29},{6,30},{7,31},{8,16},{9,... | collective-permute-start | bytes 98312 | tf_op jit(solution)/shard_map/ppermute | solution.py:28
  41.0 5.8 %collective-permute-start.10 = (s32[64,128]{1,0:T(8,128)S(1)}, s32[64,128]{1,0:T(8,128)S(1)}, u32[]{:S(2)}, u32[]{:S(2)}) collective-permute-start(s32[64,128]{1,0:T(8,128)S(1)} %dynamic-slice_add_fusion.2), channel_id=1, source_target_pairs={{0,16},{1,17},{2,18},{3,19},{4,20},{5,21},{6,22},{7,23},{8,24},{9,... | collective-permute-start | bytes 98312 | tf_op jit(solution)/shard_map/ppermute | solution.py:28
  41.6 5.1 %collective-permute-start.9 = (s32[64,128]{1,0:T(8,128)S(1)}, s32[64,128]{1,0:T(8,128)S(1)}, u32[]{:S(2)}, u32[]{:S(2)}) collective-permute-start(s32[64,128]{1,0:T(8,128)S(1)} %dynamic-slice_add_fusion.2), channel_id=1, source_target_pairs={{0,8},{1,9},{2,10},{3,11},{4,12},{5,13},{6,14},{7,15},{8,0},{9,1},... | collective-permute-start | bytes 98312 | tf_op jit(solution)/shard_map/ppermute | solution.py:28
  49.8 11.0 %collective-permute-start.16 = (bf16[2048,512]{1,0:T(8,128)(2,1)}, bf16[2048,512]{1,0:T(8,128)(2,1)}, u32[]{:S(2)}, u32[]{:S(2)}) collective-permute-start(bf16[2048,512]{1,0:T(8,128)(2,1)} %collective-permute-done.12.refs_6_.refs_2_), channel_id=1, source_target_pairs={{0,1},{1,0},{2,3},{3,2},{4,5},{5,4},{6,7},{7,6},{8,9},{9,8},{10,11... | collective-permute-start | bytes 6291464 | tf_op jit(solution)/shard_map/ppermute | solution.py:28
  49.8 12.7 %collective-permute-start.18 = (bf16[2048,512]{1,0:T(8,128)(2,1)S(1)}, bf16[2048,512]{1,0:T(8,128)(2,1)}, u32[]{:S(2)}, u32[]{:S(2)}) collective-permute-start(bf16[2048,512]{1,0:T(8,128)(2,1)S(1)} %bitcast.10), channel_id=1, source_target_pairs={{0,1},{1,0},{2,3},{3,2},{4,5},{5,4},{6,7},{7,6},{8,9},{9,8},{10,11... | collective-permute-start | bytes 6291464 | tf_op jit(solution)/shard_map/ppermute | solution.py:28
  50.3 37.6 %collective-permute-start.20 = (bf16[1536,512]{1,0:T(8,128)(2,1)}, bf16[1536,512]{1,0:T(8,128)(2,1)}, u32[]{:S(2)}, u32[]{:S(2)}) collective-permute-start(bf16[1536,512]{1,0:T(8,128)(2,1)} %get-tuple-element.91), channel_id=1, source_target_pairs={{0,2},{1,3},{2,0},{3,1},{4,6},{5,7},{6,4},{7,5},{8,10},{9,11},{10,... | collective-permute-start | bytes 4718600 | tf_op jit(solution)/shard_map/ppermute | solution.py:28
  50.9 5.7 %collective-permute-start.15 = (s32[64,128]{1,0:T(8,128)S(1)}, s32[64,128]{1,0:T(8,128)S(1)}, u32[]{:S(2)}, u32[]{:S(2)}) collective-permute-start(s32[64,128]{1,0:T(8,128)S(1)} %add_add_fusion.1), channel_id=1, source_target_pairs={{0,96},{1,97},{2,98},{3,99},{4,100},{5,101},{6,102},{7,103},{8,104... | collective-permute-start | bytes 98312 | tf_op jit(solution)/shard_map/ppermute | solution.py:28
  52.8 4.8 %collective-permute-start.14 = (s32[64,128]{1,0:T(8,128)S(1)}, s32[64,128]{1,0:T(8,128)S(1)}, u32[]{:S(2)}, u32[]{:S(2)}) collective-permute-start(s32[64,128]{1,0:T(8,128)S(1)} %add_add_fusion.1), channel_id=1, source_target_pairs={{0,64},{1,65},{2,66},{3,67},{4,68},{5,69},{6,70},{7,71},{8,72},{9,... | collective-permute-start | bytes 98312 | tf_op jit(solution)/shard_map/ppermute | solution.py:28
  56.6 4.2 %collective-permute-start.13 = (s32[64,128]{1,0:T(8,128)S(1)}, s32[64,128]{1,0:T(8,128)S(1)}, u32[]{:S(2)}, u32[]{:S(2)}) collective-permute-start(s32[64,128]{1,0:T(8,128)S(1)} %add_add_fusion.1), channel_id=1, source_target_pairs={{0,32},{1,33},{2,34},{3,35},{4,36},{5,37},{6,38},{7,39},{8,40},{9,... | collective-permute-start | bytes 98312 | tf_op jit(solution)/shard_map/ppermute | solution.py:28
  60.8 12.3 %collective-permute-start.17 = (s32[256,128]{1,0:T(8,128)S(1)}, s32[256,128]{1,0:T(8,128)S(1)}, u32[]{:S(2)}, u32[]{:S(2)}) collective-permute-start(s32[256,128]{1,0:T(8,128)S(1)} %add_select_fusion.4), channel_id=1, source_target_pairs={{0,128},{1,129},{2,130},{3,131},{4,132},{5,133},{6,134},{7,135},{8... | collective-permute-start | bytes 393224 | tf_op jit(solution)/shard_map/ppermute | solution.py:28
  60.9 37.2 %collective-permute-start.19 = (bf16[512,512]{1,0:T(8,128)(2,1)S(1)}, bf16[512,512]{1,0:T(8,128)(2,1)S(1)}, u32[]{:S(2)}, u32[]{:S(2)}) collective-permute-start(bf16[512,512]{1,0:T(8,128)(2,1)S(1)} %copy-done.10), channel_id=1, source_target_pairs={{0,2},{1,3},{2,0},{3,1},{4,6},{5,7},{6,4},{7,5},{8,10},{9,11},{10,... | collective-permute-start | bytes 1572872 | tf_op jit(solution)/shard_map/ppermute | solution.py:28
  84.1 8.0 %copy-start.2 = (f32[1536,128]{1,0:T(8,128)S(1)}, f32[1536,128]{1,0:T(8,128)}, u32[]{:S(2)}) copy-start(f32[1536,128]{1,0:T(8,128)} %param.15) | copy-start | bytes 2359300
  84.1 8.0 %copy-start.4 = (f32[1536,128]{1,0:T(8,128)S(1)}, f32[1536,128]{1,0:T(8,128)}, u32[]{:S(2)}) copy-start(f32[1536,128]{1,0:T(8,128)} %param.17) | copy-start | bytes 2359300
  98.1 0.8 copy-start.9

commit v2 on v1

--- a/solution.py
+++ b/solution.py
@@ -151,150 +151,138 @@
         out_specs=pl.BlockSpec((1, block, width), lambda g: (0, first // block + g, 0)),
         out_shape=jax.ShapeDtypeStruct((1, cuts[-1], width), bf16),
         input_output_aliases={} if so_far is None else {2: 0},
-        compiler_params=params(),
+        compiler_params=params(8),
         cost_estimate=small,
         name="add",
     )(*args)
 
 
-def weight_specs(rows, block, width):
-    specs = []
-    first = 0
-    for count in rows:
-        steps = count // block
-
-        def index(i, *_, first=first, steps=steps):
-            return (jnp.clip(i - first, 0, steps - 1), 0)
-
-        specs.append(pl.BlockSpec((block, width), index))
-        first += steps
-    return specs
-
-
-def at_step(step, rows, block, refs, body):
-    first = 0
-    for count, ref in zip(rows, refs, strict=True):
-        last = first + count // block
-
-        @pl.when((step >= first) & (step < last))
-        def _(ref=ref):
-            body(ref)
-
-        first = last
-
-
-def keys_kernel(near_ref, *refs, rows, block, width):
-    far = refs[:4]
-    weights = refs[4 : 4 + len(rows)]
-    cot_ref, inv_ref, keys_ref, factor_ref, total_ref = refs[4 + len(rows) :]
-    step = pl.program_id(0)
-    per = width // 4 // block
-
-    @pl.when(step == 0)
-    def _():
-        total_ref[...] = jnp.zeros_like(total_ref)
-
-    def near_body(w_ref):
-        total_ref[...] += jnp.dot(near_ref[0], w_ref[...], preferred_element_type=f32)
-
-    def far_body(w_ref):
-        for k, part_ref in enumerate(far):
-
-            @pl.when(step == per * (1 + 2 * (k // per)) + k % per)
-            def _(part_ref=part_ref):
-                total_ref[...] += jnp.dot(part_ref[...], w_ref[...], preferred_element_type=f32)
-
-    is_near = (step // per) % 2 == 0
-
-    @pl.when(is_near)
-    def _():
-        at_step(step, rows, block, weights, near_body)
-
-    @pl.when(jnp.logical_not(is_near))
-    def _():
-        at_step(step, rows, block, weights, far_body)
-
-    @pl.when(step == 4 * per - 1)
-    def _():
-        keys = total_ref[...]
-        keys_ref[...] = keys.astype(bf16)
-        dots = jnp.sum(cot_ref[...].astype(f32) * keys, axis=1, keepdims=True) / width
-        inv = inv_ref[...]
-        factor_ref[...] = inv * inv * dots
-
-
-def keys_of(near, far, weights, cot, inv):
+pieces = 4
+
+
+def token_kernel(me_ref, near_hbm, *refs):
+    far_hbm = refs[:4]
+    whole_hbm = refs[4:7]
+    piece_hbm = refs[7 : 7 + pieces]
+    x_hbm, gain_ref, cot_ref, inv_ref, keys_ref, out_hbm = refs[7 + pieces : 13 + pieces]
+    near, far, w, x, out, sems, out_sems = refs[13 + pieces :]
     _, tokens, slab = near.shape
-    width = cot.shape[1]
-    per = 2
-    block = slab // per
-    rows = [w.shape[0] for w in weights]
-
-    def near_place(i):
-        late = i >= 2 * per
-        return (late.astype(jnp.int32), 0, jnp.minimum(jnp.where(late, i - 2 * per, i), per - 1))
-
-    fixed = lambda i: (0, 0)
+    half = slab // 2
+    width = 4 * slab
+    me = me_ref[0]
+    used = []
+
+    def load(source, target):
+        copy = pltpu.make_async_copy(source, target, sems.at[len(used)])
+        used.append(copy)
+        copy.start()
+        return copy
+
+    def column(s, h):
+        return pl.multiple_of((me ^ s) * slab + h * half, half)
+
+    waits = []
+    for s in range(4):
+        group = []
+        if s % 2 == 0:
+            group.append(load(near_hbm.at[s // 2], near.at[s // 2]))
+        else:
+            for k in (s - 1, s):
+                group.append(load(far_hbm[k], far.at[k]))
+        if s < 3:
+            group.append(load(whole_hbm[s], w.at[s]))
+        else:
+            rows = slab // pieces
+            for k in range(pieces):
+                group.append(load(piece_hbm[k], w.at[s, pl.ds(k * rows, rows)]))
+        waits.append(group)
+    x_waits = [load(x_hbm.at[:, pl.ds(column(s, 0), slab)], x.at[s]) for s in range(4)]
+
+    keys = jnp.zeros(keys_ref.shape, f32)
+    for s in range(4):
+        for copy in waits[s]:
+            copy.wait()
+        if s % 2 == 0:
+            keys = keys + jnp.dot(near[s // 2], w[s], preferred_element_type=f32)
+        else:
+            for h in range(2):
+                part = w[s, h * half : (h + 1) * half, :]
+                keys = keys + jnp.dot(far[s - 1 + h], part, preferred_element_type=f32)
+    keys_ref[...] = keys.astype(bf16)
+    cot = cot_ref[...]
+    inv = inv_ref[:, :1]
+    factor = inv * inv * (jnp.sum(cot.astype(f32) * keys, axis=1, keepdims=True) / width)
+
+    sent = []
+    for s in range(4):
+        x_waits[s].wait()
+        for h in range(2):
+            part = w[s, h * half : (h + 1) * half, :]
+            dnormed = lax.dot_general(cot, part, (((1,), (1,)), ((), ())), preferred_element_type=f32)
+            scaled = gain_ref[:, pl.ds(column(s, h), half)] * dnormed
+            values = x[s, :, h * half : (h + 1) * half].astype(f32)
+            out[s, h] = (inv * scaled - values * factor).astype(bf16)
+            copy = pltpu.make_async_copy(
+                out.at[s, h], out_hbm.at[:, pl.ds(column(s, h), half)], out_sems.at[2 * s + h]
+            )
+            copy.start()
+            sent.append(copy)
+    for copy in sent:
+        copy.wait()
+
+
+def token_outputs(me, near, far, whole, parts, hidden, gain, cot, inv):
+    tokens, width = hidden.shape
+    slab = width // 4
+    keys_width = cot.shape[1]
+    far_off = pl.BlockSpec(memory_space=pl.ANY)
+    close = pl.BlockSpec(memory_space=pltpu.VMEM)
+    loads = 2 + 4 + 3 + pieces + 4
     return pl.pallas_call(
-        functools.partial(keys_kernel, rows=rows, block=block, width=4 * slab),
-        grid=(4 * per,),
-        in_specs=[pl.BlockSpec((1, tokens, block), near_place)]
-        + [pl.BlockSpec((tokens, block), fixed)] * 4
-        + weight_specs(rows, block, width)
-        + [pl.BlockSpec((tokens, width), fixed), pl.BlockSpec((tokens, 128), fixed)],
-        out_specs=[pl.BlockSpec((tokens, width), fixed), pl.BlockSpec((tokens, 128), fixed)],
-        out_shape=[jax.ShapeDtypeStruct((tokens, width), bf16), jax.ShapeDtypeStruct((tokens, 128), f32)],
-        scratch_shapes=[pltpu.VMEM((tokens, width), f32)],
+        token_kernel,
+        in_specs=[pl.BlockSpec(memory_space=pltpu.SMEM)] + [far_off] * (9 + pieces) + [close] * 3,
+        out_specs=[close, far_off],
+        out_shape=[
+            jax.ShapeDtypeStruct((tokens, keys_width), bf16),
+            jax.ShapeDtypeStruct((tokens, width), bf16),
+        ],
+        scratch_shapes=[
+            pltpu.VMEM((2, tokens, slab), bf16),
+            pltpu.VMEM((4, tokens, slab // 2), bf16),
+            pltpu.VMEM((4, slab, keys_width), bf16),
+            pltpu.VMEM((4, tokens, slab), bf16),
+            pltpu.VMEM((4, 2, tokens, slab // 2), bf16),
+            pltpu.SemaphoreType.DMA((loads,)),
+            pltpu.SemaphoreType.DMA((8,)),
+        ],
         compiler_params=params(),
         cost_estimate=small,
-        name="keys",
-    )(near, *far, *weights, cot, inv)
-
-
-def input_kernel(me_ref, x_ref, gain_ref, *refs, rows, block):
-    weights = refs[: len(rows)]
-    cot_ref, inv_ref, factor_ref, out_ref = refs[len(rows) :]
-
-    def body(w_ref):
-        dnormed = lax.dot_general(
-            cot_ref[...], w_ref[...], (((1,), (1,)), ((), ())), preferred_element_type=f32
-        )
-        scaled = gain_ref[...] * dnormed
-        out_ref[...] = (inv_ref[:, :1] * scaled - x_ref[...].astype(f32) * factor_ref[:, :1]).astype(bf16)
-
-    at_step(pl.program_id(0), rows, block, weights, body)
-
-
-def input_grad_of(me, hidden, gain, weights, cot, inv, factor):
-    tokens, total = hidden.shape
-    width = cot.shape[1]
-    per = 2
-    block = total // 4 // per
-    rows = [w.shape[0] for w in weights]
-
-    def column(i, m):
-        return (0, (m[0] ^ (i // per)) * per + i % per)
-
-    fixed = lambda i, m: (0, 0)
+        name="keys_and_input_grad",
+    )(me, near, *far, *whole, *parts, hidden, gain, cot, inv)
+
+
+def split_kernel(source, *targets):
+    rows = targets[0].shape[0]
+    for k, target in enumerate(targets):
+
+        @pl.when(pl.program_id(0) == k)
+        def _(target=target):
+            target[...] = source[...]
+
+
+def in_pieces(value):
+    rows, width = value.shape
+    rows = rows // pieces
     return pl.pallas_call(
-        functools.partial(input_kernel, rows=rows, block=block),
-        grid_spec=pltpu.PrefetchScalarGridSpec(
-            num_scalar_prefetch=1,
-            grid=(4 * per,),
-            in_specs=[pl.BlockSpec((tokens, block), column), pl.BlockSpec((1, block), column)]
-            + weight_specs(rows, block, width)
-            + [
-                pl.BlockSpec((tokens, width), fixed),
-                pl.BlockSpec((tokens, 128), fixed),
-                pl.BlockSpec((tokens, 128), fixed),
-            ],
-            out_specs=pl.BlockSpec((tokens, block), column),
-        ),
-        out_shape=jax.ShapeDtypeStruct((tokens, total), bf16),
+        split_kernel,
+        grid=(pieces,),
+        in_specs=[pl.BlockSpec((rows, width), lambda i: (i, 0))],
+        out_specs=[pl.BlockSpec((rows, width), lambda i: (0, 0))] * pieces,
+        out_shape=[pltpu.HBM((rows, width), value.dtype)] * pieces,
         compiler_params=params(),
         cost_estimate=small,
-        name="input_grad",
-    )(me, hidden, gain, *weights, cot, inv, factor)
+        name="split",
+    )(value)
 
 
 def packed_codes(global_base, replica_params, level, dither_seeds, fragment_index):
@@ -391,20 +379,23 @@
     )
     in_rows = [send(rows, x_lo_bit) for rows in out_rows]
     total, _ = halve(total, 1, nothing)
-    total, own_rows = exchange(
+    total, _ = exchange(total, (y_bit, y_bit * 2, y_bit * 3), nothing)
+    total, partner = lax.optimization_barrier((total, partner))
+    diagonal = [send(part, core_bit) for part in in_pieces(partner)]
+    total, (diagonal, own_rows) = rejoin_four(
         total,
-        (y_bit, y_bit * 2, y_bit * 3),
-        lambda: grad_rows(near, came, key_cot, cot_sibling, 0, f32, "grad_own"),
-    )
-    total, partner = lax.optimization_barrier((total, partner))
-    diagonal = send(partner, core_bit)
-    total, diagonal = rejoin_four(total, lambda: diagonal)
-    weights = (own, sibling, partner, diagonal)
-    total, (keys, factor) = rejoin(total, 4, lambda: keys_of(near, far, weights, key_cot, inv))
+        lambda: (diagonal, grad_rows(near, came, key_cot, cot_sibling, 0, f32, "grad_own")),
+    )
+    total, (keys, input_grad) = rejoin(
+        total,
+        4,
+        lambda: token_outputs(
+            me, near, far, (own, sibling, partner), diagonal, hidden, gain, key_cot, inv
+        ),
+    )
     new_base, new_momentum = outer_update(
         total, global_base, outer_momentum, level, lax.axis_size("rep")
     )
-    input_grad = input_grad_of(me, hidden, gain, weights, key_cot, inv, factor)
     input_grad, in_rows[0] = lax.optimization_barrier((input_grad, in_rows[0]))
     weight_grad = None
     for first, own_part, in_part in zip(cuts, own_rows, in_rows):

time: 103 us -> 95.9 us (0.931); the launches traced: 101 us -> 95.6 us
  Pallas kernels: 42.5 us -> 32.4 us
  waiting for transfers between devices: 31 us -> 36.2 us
    pallas_call x2, Pallas kernels: 21.6 us -> 15.1 us  [the longest x1 11.4 us: token_outputs(): pl.pallas_call(token_kernel, in_specs=[pl.BlockSpec(memory_space=pltpu.SM...]
    ppermute x21 -> x24, waiting for transfers between devices: 31 us -> 36.2 us  [send(): return lax.ppermute(value, axes, flip(bit))]
    pallas_call x2, Pallas kernels: 6.41 us -> 2.67 us  [add_rows(): pl.pallas_call(add_kernel, grid=(rows // block,), in_specs=[part, part] +...]
    ppermute x21 -> x24, starting transfers between devices: 18 us -> 18.2 us  [send(): return lax.ppermute(value, axes, flip(bit))]
  transfers between devices with their start and end apart: 21 -> 24, of which waited for: 10 -> 12; matrix products, arithmetic and copies ran while one was open for 7% -> 7% of each run, Pallas kernels for 40% -> 33%
where the time goes in v2:
time: 95.9 us; the launch traced here: 95.6 us
  waiting for transfers between devices  36.2 us (38%)
  Pallas kernels  32.4 us (34%)
  starting transfers between devices  18.2 us (19%)
  other arithmetic  6.56 us (7%)
  between operations  1.53 us (2%)
    ppermute x24, waiting for transfers between devices, send(): return lax.ppermute(value, axes, flip(bit))  36.2 us
    ppermute x24, starting transfers between devices, send(): return lax.ppermute(value, axes, flip(bit))  18.2 us
    pallas_call x1, Pallas kernels, token_outputs(): pl.pallas_call(token_kernel, in_specs=[pl.BlockSpec(memory_space=pltpu.SM...  11.4 us
    pallas_call x2, Pallas kernels, grad_rows(): pl.pallas_call(grad_kernel, grid=(1,), in_specs=[pl.BlockSpec((1, tokens,...  8.74 us
    pallas_call x1, Pallas kernels, norm_slabs(): pl.pallas_call(norm_kernel, grid_spec=pltpu.PrefetchScalarGridSpec(num_sc...  5.88 us
    pallas_call x1, Pallas kernels, in_pieces(): pl.pallas_call(split_kernel, grid=(pieces,), in_specs=[pl.BlockSpec((rows...  3.7 us
    add x1, other arithmetic, packed_codes(): shifted = code + 8  3.39 us
    pallas_call x2, Pallas kernels, add_rows(): pl.pallas_call(add_kernel, grid=(rows // block,), in_specs=[part, part] +...  2.67 us
  transfers between devices with their start and end apart: 24, of which 12 were waited for; matrix products, arithmetic and copies ran while one was open for 7% of the time, Pallas kernels for 33%

profile of v2, /device:TPU:130, one launch (start us, length us, event | category | flops | bytes accessed | tf_op | source)
XLA Modules:
  0.0 95.6 jit_solution(7843897294923433643)
XLA Ops:
  0.6 0.6 collective-permute-start.12
  1.9 0.7 reduce
  2.6 0.8 select_reduce_fusion
  3.4 3.4 %fusion.10 = s32[1536,128]{1,0:T(8,128)S(1)} fusion(f32[1536,128]{1,0:T(8,128)} %param.15, bf16[1,1536,128]{2,1,0:T(8,128)(2,1)} %param.16, s32[]{:T(128)} %bitcast.1, s32[128]{0:T(128)S(1)} %iota_multiply_fusion, s32[1536]{0:T(1024)S(1)} %reduce, f32[1536]{0:T(1024)S(1)} %select_reduce_fusion), kind=kLoop, calls=%fused_computation.16 | loop fusion | flops 7667712 | bytes 1978884 | tf_op jit(solution)/shard_map/add | solution.py:294
  7.5 5.9 %norm.1 = (bf16[2,256,2048]{2,1,0:T(8,128)(2,1)}, bf16[256,1024]{1,0:T(8,128)(2,1)}, bf16[256,1024]{1,0:T(8,128)(2,1)}, bf16[256,1024]{1,0:T(8,128)(2,1)}, bf16[...) custom-call(s32[1]{0:T(128)} %bitcast.2.me_ref, bf16[256,8192]{1,0:T(8,128)(2,1)} %refs_11_, f32[1,8192]{1,0:T(1,128)} %bitcast.7), custom_call_target="tpu_custom_call" | custom-call | flops 1024 | bytes 1024 | tf_op jit(solution)/shard_map/norm/pallas_call | solution.py:78
  13.4 4.6 %collective-permute-done = s32[256,128]{1,0:T(8,128)S(1)} collective-permute-done((s32[256,128]{1,0:T(8,128)S(1)}, s32[256,128]{1,0:T(8,128)S(1)}, u32[]{:S(2)}, u32[]{:S(2)}) %collective-permute-start) | collective-permute-done | bytes 131104 | tf_op jit(solution)/shard_map/ppermute | solution.py:28
  18.0 2.2 %collective-permute-start.1 = (s32[128,128]{1,0:T(8,128)S(1)}, s32[128,128]{1,0:T(8,128)S(1)}, u32[]{:S(2)}, u32[]{:S(2)}) collective-permute-start(s32[128,128]{1,0:T(8,128)S(1)} %constant_dynamic-slice_fusion.1), channel_id=1, source_target_pairs={{0,64},{1,65},{2,66},{3,67},{4,68},{5,69},{6,70},{7,71},{8,72},{9,... | collective-permute-start | bytes 196616 | tf_op jit(solution)/shard_map/ppermute | solution.py:28
  20.7 2.6 %collective-permute-done.1 = s32[128,128]{1,0:T(8,128)S(1)} collective-permute-done((s32[128,128]{1,0:T(8,128)S(1)}, s32[128,128]{1,0:T(8,128)S(1)}, u32[]{:S(2)}, u32[]{:S(2)}) %collective-permute-start.1) | collective-permute-done | bytes 65568 | tf_op jit(solution)/shard_map/ppermute | solution.py:28
  23.9 1.5 %collective-permute-done.5.high_ref = bf16[256,1024]{1,0:T(8,128)(2,1)S(1)} collective-permute-done((bf16[256,1024]{1,0:T(8,128)(2,1)}, bf16[256,1024]{1,0:T(8,128)(2,1)S(1)}, u32[]{:S(2)}, u32[]{:S(2)}) %collective-permute-start.5) | collective-permute-done | bytes 524320 | tf_op jit(solution)/shard_map/ppermute | solution.py:28
  25.4 3.6 %collective-permute-start.6 = (s32[128,128]{1,0:T(8,128)S(1)}, s32[128,128]{1,0:T(8,128)S(1)}, u32[]{:S(2)}, u32[]{:S(2)}) collective-permute-start(s32[128,128]{1,0:T(8,128)S(1)} %dynamic-slice_add_fusion.1), channel_id=1, source_target_pairs={{0,36},{1,37},{2,38},{3,39},{4,32},{5,33},{6,34},{7,35},{8,44},{9,... | collective-permute-start | bytes 196616 | tf_op jit(solution)/shard_map/ppermute | solution.py:28
  29.1 0.7 copy-done.4
  29.8 4.1 %grad_out.1 = (bf16[1536,512]{1,0:T(8,128)(2,1)}, bf16[512,512]{1,0:T(8,128)(2,1)}) custom-call(bf16[2,256,2048]{2,1,0:T(8,128)(2,1)} %get-tuple-element.71.mine_ref.near_hbm, bf16[256,1024]{1,0:T(8,128)(2,1)} %copy-done.8, bf16[256,1024]{1,0:T(8,128)(2,1)} %copy-done.9, bf16[256,512]{1,0:T(8,128)(2,1)} %refs_13_.1, bf16[256,512]{1,0:T(8,128)(2,1)} %copy-done.4), custom_call_target="tpu_custom_call" | custom-call | flops 1024 | bytes 1024 | tf_op jit(solution)/shard_map/grad_out/pallas_call | solution.py:120
  34.3 3.6 %collective-permute-done.8 = s32[64,128]{1,0:T(8,128)S(1)} collective-permute-done((s32[64,128]{1,0:T(8,128)S(1)}, s32[64,128]{1,0:T(8,128)S(1)}, u32[]{:S(2)}, u32[]{:S(2)}) %collective-permute-start.8) | collective-permute-done | bytes 32800 | tf_op jit(solution)/shard_map/ppermute | solution.py:28
  37.9 3.0 %collective-permute-start.11 = (s32[64,128]{1,0:T(8,128)S(1)}, s32[64,128]{1,0:T(8,128)S(1)}, u32[]{:S(2)}, u32[]{:S(2)}) collective-permute-start(s32[64,128]{1,0:T(8,128)S(1)} %dynamic-slice_add_fusion.2), channel_id=1, source_target_pairs={{0,24},{1,25},{2,26},{3,27},{4,28},{5,29},{6,30},{7,31},{8,16},{9,... | collective-permute-start | bytes 98312 | tf_op jit(solution)/shard_map/ppermute | solution.py:28
  40.9 0.6 collective-permute-start.10
  42.0 1.0 %collective-permute-done.11 = s32[64,128]{1,0:T(8,128)S(1)} collective-permute-done((s32[64,128]{1,0:T(8,128)S(1)}, s32[64,128]{1,0:T(8,128)S(1)}, u32[]{:S(2)}, u32[]{:S(2)}) %collective-permute-start.11) | collective-permute-done | bytes 32800 | tf_op jit(solution)/shard_map/ppermute | solution.py:28
  43.1 1.8 %collective-permute-start.23 = (bf16[1536,512]{1,0:T(8,128)(2,1)}, bf16[1536,512]{1,0:T(8,128)(2,1)S(1)}, u32[]{:S(2)}, u32[]{:S(2)}) collective-permute-start(bf16[1536,512]{1,0:T(8,128)(2,1)} %get-tuple-element.105), channel_id=1, source_target_pairs={{0,2},{1,3},{2,0},{3,1},{4,6},{5,7},{6,4},{7,5},{8,10},{9,11},{10,... | collective-permute-start | bytes 4718600 | tf_op jit(solution)/shard_map/ppermute | solution.py:28
  44.9 1.5 %collective-permute-done.10 = s32[64,128]{1,0:T(8,128)S(1)} collective-permute-done((s32[64,128]{1,0:T(8,128)S(1)}, s32[64,128]{1,0:T(8,128)S(1)}, u32[]{:S(2)}, u32[]{:S(2)}) %collective-permute-start.10) | collective-permute-done | bytes 32800 | tf_op jit(solution)/shard_map/ppermute | solution.py:28
  46.4 4.6 %collective-permute-done.12.source.refs_6_ = bf16[2048,512]{1,0:T(8,128)(2,1)} collective-permute-done((bf16[2048,512]{1,0:T(8,128)(2,1)}, bf16[2048,512]{1,0:T(8,128)(2,1)}, u32[]{:S(2)}, u32[]{:S(2)}) %collective-permute-start.12) | collective-permute-done | bytes 2097184 | tf_op jit(solution)/shard_map/ppermute | solution.py:28
  51.0 3.7 %split.1 = (bf16[512,512]{1,0:T(8,128)(2,1)}, bf16[512,512]{1,0:T(8,128)(2,1)}, bf16[512,512]{1,0:T(8,128)(2,1)}, bf16[512,512]{1,0:T(8,128)(2,1)}) custom-call(bf16[2048,512]{1,0:T(8,128)(2,1)} %collective-permute-done.12.source.refs_6_), custom_call_target="tpu_custom_call" | custom-call | flops 1024 | bytes 1024 | tf_op jit(solution)/shard_map/split/pallas_call | solution.py:276
  54.7 1.9 %collective-permute-start.15 = (s32[64,128]{1,0:T(8,128)S(1)}, s32[64,128]{1,0:T(8,128)S(1)}, u32[]{:S(2)}, u32[]{:S(2)}) collective-permute-start(s32[64,128]{1,0:T(8,128)S(1)} %add_add_fusion.1), channel_id=1, source_target_pairs={{0,96},{1,97},{2,98},{3,99},{4,100},{5,101},{6,102},{7,103},{8,104... | collective-permute-start | bytes 98312 | tf_op jit(solution)/shard_map/ppermute | solution.py:28
  57.1 3.5 %collective-permute-done.15 = s32[64,128]{1,0:T(8,128)S(1)} collective-permute-done((s32[64,128]{1,0:T(8,128)S(1)}, s32[64,128]{1,0:T(8,128)S(1)}, u32[]{:S(2)}, u32[]{:S(2)}) %collective-permute-start.15) | collective-permute-done | bytes 32800 | tf_op jit(solution)/shard_map/ppermute | solution.py:28
  60.6 1.0 %collective-permute-done.14 = s32[64,128]{1,0:T(8,128)S(1)} collective-permute-done((s32[64,128]{1,0:T(8,128)S(1)}, s32[64,128]{1,0:T(8,128)S(1)}, u32[]{:S(2)}, u32[]{:S(2)}) %collective-permute-start.14) | collective-permute-done | bytes 32800 | tf_op jit(solution)/shard_map/ppermute | solution.py:28
  61.7 2.9 %collective-permute-done.13 = s32[64,128]{1,0:T(8,128)S(1)} collective-permute-done((s32[64,128]{1,0:T(8,128)S(1)}, s32[64,128]{1,0:T(8,128)S(1)}, u32[]{:S(2)}, u32[]{:S(2)}) %collective-permute-start.13) | collective-permute-done | bytes 32800 | tf_op jit(solution)/shard_map/ppermute | solution.py:28
  65.1 4.7 %grad_own.1 = (f32[1536,512]{1,0:T(8,128)}, f32[512,512]{1,0:T(8,128)}) custom-call(bf16[2,256,2048]{2,1,0:T(8,128)(2,1)} %get-tuple-element.71.mine_ref.near_hbm, bf16[256,1024]{1,0:T(8,128)(2,1)} %copy-done.6, bf16[256,1024]{1,0:T(8,128)(2,1)} %copy-done.7, bf16[256,512]{1,0:T(8,128)(2,1)} %refs_13_.1, bf16[256,512]{1,0:T(8,128)(2,1)} %copy-done.4), custom_call_target="tpu_custom_call" | custom-call | flops 1024 | bytes 1024 | tf_op jit(solution)/shard_map/grad_own/pallas_call | solution.py:120
  69.9 0.6 collective-permute-start.22
  70.5 11.4 %keys_and_input_grad.1 = (bf16[256,512]{1,0:T(8,128)(2,1)}, bf16[256,8192]{1,0:T(8,128)(2,1)}) custom-call(s32[1]{0:T(128)} %bitcast.2.me_ref, bf16[2,256,2048]{2,1,0:T(8,128)(2,1)} %get-tuple-element.71.mine_ref.near_hbm, bf16[256,1024]{1,0:T(8,128)(2,1)} %get-tuple-element.66.refs_0_, bf16[256,1024]{1,0:T(8,128)(2,1)} %get-tuple-element.67.refs_1_, ...), custom_call_target="tpu_custom_call" | custom-call | flops 1024 | bytes 1024 | tf_op jit(solution)/shard_map/keys_and_input_grad/pallas_call | solution.py:241
  82.0 2.6 %collective-permute-done.23.came_ref = bf16[1536,512]{1,0:T(8,128)(2,1)S(1)} collective-permute-done((bf16[1536,512]{1,0:T(8,128)(2,1)}, bf16[1536,512]{1,0:T(8,128)(2,1)S(1)}, u32[]{:S(2)}, u32[]{:S(2)}) %collective-permute-start.23) | collective-permute-done | bytes 1572896 | tf_op jit(solution)/shard_map/ppermute | solution.py:28
  84.6 1.8 %add.339.refs_0_ = bf16[1,2048,512]{2,1,0:T(8,128)(2,1)} custom-call(f32[1536,512]{1,0:T(8,128)S(1)} %copy-done, bf16[1536,512]{1,0:T(8,128)(2,1)S(1)} %collective-permute-done.23.came_ref), custom_call_target="tpu_custom_call" | custom-call | flops 1024 | bytes 1024 | tf_op jit(solution)/shard_map/add/pallas_call | solution.py:147
  86.4 1.5 %multiply_subtract_fusion = (f32[1536,128]{1,0:T(8,128)}, f32[1536,128]{1,0:T(8,128)}) fusion(f32[1536,128]{1,0:T(8,128)S(1)} %copy-done.2, s32[512,128]{1,0:T(8,128)S(1)} %get-tuple-element.113, s32[512,128]{1,0:T(8,128)S(1)} %get-tuple-element.112, s32[512,128]{1,0:T(8,128)S(1)} %get-tuple-element.111, f32[1536]{0:T(1024)S(1)} %divide_multiply_fusion, ...), kind=kLoop, calls=%fused_computation.22 | loop fusion | flops 2162688 | bytes 3938304 | tf_op jit(solution)/shard_map/sub | solution.py:346
  87.9 6.8 %collective-permute-done.22.came_ref = bf16[512,512]{1,0:T(8,128)(2,1)S(1)} collective-permute-done((bf16[512,512]{1,0:T(8,128)(2,1)}, bf16[512,512]{1,0:T(8,128)(2,1)S(1)}, u32[]{:S(2)}, u32[]{:S(2)}) %collective-permute-start.22) | collective-permute-done | bytes 524320 | tf_op jit(solution)/shard_map/ppermute | solution.py:28
  94.6 0.9 add.340
  (62 shorter events, 4.0 us)
Async XLA Ops:
  0.6 50.3 %collective-permute-start.12 = (bf16[2048,512]{1,0:T(8,128)(2,1)}, bf16[2048,512]{1,0:T(8,128)(2,1)}, u32[]{:S(2)}, u32[]{:S(2)}) collective-permute-start(bf16[2048,512]{1,0:T(8,128)(2,1)} %bitcast.4.refs_4_), channel_id=1, source_target_pairs={{0,2},{1,3},{2,0},{3,1},{4,6},{5,7},{6,4},{7,5},{8,10},{9,11},{10,... | collective-permute-start | bytes 6291464 | tf_op jit(solution)/shard_map/ppermute | solution.py:28
  6.9 11.1 %collective-permute-start = (s32[256,128]{1,0:T(8,128)S(1)}, s32[256,128]{1,0:T(8,128)S(1)}, u32[]{:S(2)}, u32[]{:S(2)}) collective-permute-start(s32[256,128]{1,0:T(8,128)S(1)} %constant_dynamic-slice_fusion.2), channel_id=1, source_target_pairs={{0,128},{1,129},{2,130},{3,131},{4,132},{5,133},{6,134},{7,135},{8... | collective-permute-start | bytes 393224 | tf_op jit(solution)/shard_map/ppermute | solution.py:28
  7.5 15.8 %copy-start.3 = (bf16[256,512]{1,0:T(8,128)(2,1)S(1)}, bf16[256,512]{1,0:T(8,128)(2,1)}, u32[]{:S(2)}) copy-start(bf16[256,512]{1,0:T(8,128)(2,1)} %refs_13_.1) | copy-start | bytes 786436
  18.0 5.3 %collective-permute-start.1 = (s32[128,128]{1,0:T(8,128)S(1)}, s32[128,128]{1,0:T(8,128)S(1)}, u32[]{:S(2)}, u32[]{:S(2)}) collective-permute-start(s32[128,128]{1,0:T(8,128)S(1)} %constant_dynamic-slice_fusion.1), channel_id=1, source_target_pairs={{0,64},{1,65},{2,66},{3,67},{4,68},{5,69},{6,70},{7,71},{8,72},{9,... | collective-permute-start | bytes 196616 | tf_op jit(solution)/shard_map/ppermute | solution.py:28
  20.2 3.1 %collective-permute-start.2 = (bf16[256,1024]{1,0:T(8,128)(2,1)}, bf16[256,1024]{1,0:T(8,128)(2,1)S(1)}, u32[]{:S(2)}, u32[]{:S(2)}) collective-permute-start(bf16[256,1024]{1,0:T(8,128)(2,1)} %get-tuple-element.66.refs_0_), channel_id=1, source_target_pairs={{0,1},{1,0},{2,3},{3,2},{4,5},{5,4},{6,7},{7,6},{8,9},{9,8},{10,11... | collective-permute-start | bytes 1572872 | tf_op jit(solution)/shard_map/ppermute | solution.py:28
  20.2 3.7 %collective-permute-start.3 = (bf16[256,1024]{1,0:T(8,128)(2,1)}, bf16[256,1024]{1,0:T(8,128)(2,1)S(1)}, u32[]{:S(2)}, u32[]{:S(2)}) collective-permute-start(bf16[256,1024]{1,0:T(8,128)(2,1)} %get-tuple-element.67.refs_1_), channel_id=1, source_target_pairs={{0,1},{1,0},{2,3},{3,2},{4,5},{5,4},{6,7},{7,6},{8,9},{9,8},{10,11... | collective-permute-start | bytes 1572872 | tf_op jit(solution)/shard_map/ppermute | solution.py:28
  20.7 3.2 %collective-permute-start.4 = (bf16[256,1024]{1,0:T(8,128)(2,1)}, bf16[256,1024]{1,0:T(8,128)(2,1)S(1)}, u32[]{:S(2)}, u32[]{:S(2)}) collective-permute-start(bf16[256,1024]{1,0:T(8,128)(2,1)} %get-tuple-element.68.refs_2_), channel_id=1, source_target_pairs={{0,1},{1,0},{2,3},{3,2},{4,5},{5,4},{6,7},{7,6},{8,9},{9,8},{10,11... | collective-permute-start | bytes 1572872 | tf_op jit(solution)/shard_map/ppermute | solution.py:28
  23.3 2.1 %collective-permute-start.5 = (bf16[256,1024]{1,0:T(8,128)(2,1)}, bf16[256,1024]{1,0:T(8,128)(2,1)S(1)}, u32[]{:S(2)}, u32[]{:S(2)}) collective-permute-start(bf16[256,1024]{1,0:T(8,128)(2,1)} %get-tuple-element.69.refs_3_), channel_id=1, source_target_pairs={{0,1},{1,0},{2,3},{3,2},{4,5},{5,4},{6,7},{7,6},{8,9},{9,8},{10,11... | collective-permute-start | bytes 1572872 | tf_op jit(solution)/shard_map/ppermute | solution.py:28
  23.3 41.8 %copy-start.6 = (bf16[256,1024]{1,0:T(8,128)(2,1)}, bf16[256,1024]{1,0:T(8,128)(2,1)S(1)}, u32[]{:S(2)}) copy-start(bf16[256,1024]{1,0:T(8,128)(2,1)S(1)} %collective-permute-done.2.low_ref) | copy-start | bytes 1572868
  23.3 5.8 %collective-permute-start.7 = (bf16[256,512]{1,0:T(8,128)(2,1)S(1)}, bf16[256,512]{1,0:T(8,128)(2,1)S(1)}, u32[]{:S(2)}, u32[]{:S(2)}) collective-permute-start(bf16[256,512]{1,0:T(8,128)(2,1)S(1)} %copy-done.3), channel_id=1, source_target_pairs={{0,1},{1,0},{2,3},{3,2},{4,5},{5,4},{6,7},{7,6},{8,9},{9,8},{10,11... | collective-permute-start | bytes 786440 | tf_op jit(solution)/shard_map/ppermute | solution.py:28
  23.9 41.2 %copy-start.7 = (bf16[256,1024]{1,0:T(8,128)(2,1)}, bf16[256,1024]{1,0:T(8,128)(2,1)S(1)}, u32[]{:S(2)}) copy-start(bf16[256,1024]{1,0:T(8,128)(2,1)S(1)} %collective-permute-done.3.high_ref) | copy-start | bytes 1572868
  23.9 5.2 %copy-start.8 = (bf16[256,1024]{1,0:T(8,128)(2,1)}, bf16[256,1024]{1,0:T(8,128)(2,1)S(1)}, u32[]{:S(2)}) copy-start(bf16[256,1024]{1,0:T(8,128)(2,1)S(1)} %collective-permute-done.4.low_ref) | copy-start | bytes 1572868
  25.4 8.5 %collective-permute-start.6 = (s32[128,128]{1,0:T(8,128)S(1)}, s32[128,128]{1,0:T(8,128)S(1)}, u32[]{:S(2)}, u32[]{:S(2)}) collective-permute-start(s32[128,128]{1,0:T(8,128)S(1)} %dynamic-slice_add_fusion.1), channel_id=1, source_target_pairs={{0,36},{1,37},{2,38},{3,39},{4,32},{5,33},{6,34},{7,35},{8,44},{9,... | collective-permute-start | bytes 196616 | tf_op jit(solution)/shard_map/ppermute | solution.py:28
  29.1 41.5 %collective-permute-start.21 = (bf16[2048,512]{1,0:T(8,128)(2,1)}, bf16[2048,512]{1,0:T(8,128)(2,1)}, u32[]{:S(2)}, u32[]{:S(2)}) collective-permute-start(bf16[2048,512]{1,0:T(8,128)(2,1)} %bitcast.4.refs_4_), channel_id=1, source_target_pairs={{0,1},{1,0},{2,3},{3,2},{4,5},{5,4},{6,7},{7,6},{8,9},{9,8},{10,11... | collective-permute-start | bytes 6291464 | tf_op jit(solution)/shard_map/ppermute | solution.py:28
  33.9 4.0 %collective-permute-start.8 = (s32[64,128]{1,0:T(8,128)S(1)}, s32[64,128]{1,0:T(8,128)S(1)}, u32[]{:S(2)}, u32[]{:S(2)}) collective-permute-start(s32[64,128]{1,0:T(8,128)S(1)} %constant_dynamic-slice_fusion), channel_id=1, source_target_pairs={{0,32},{1,33},{2,34},{3,35},{4,36},{5,37},{6,38},{7,39},{8,40},{9,... | collective-permute-start | bytes 98312 | tf_op jit(solution)/shard_map/ppermute | solution.py:28
  37.9 5.1 %collective-permute-start.11 = (s32[64,128]{1,0:T(8,128)S(1)}, s32[64,128]{1,0:T(8,128)S(1)}, u32[]{:S(2)}, u32[]{:S(2)}) collective-permute-start(s32[64,128]{1,0:T(8,128)S(1)} %dynamic-slice_add_fusion.2), channel_id=1, source_target_pairs={{0,24},{1,25},{2,26},{3,27},{4,28},{5,29},{6,30},{7,31},{8,16},{9,... | collective-permute-start | bytes 98312 | tf_op jit(solution)/shard_map/ppermute | solution.py:28
  40.9 5.4 %collective-permute-start.10 = (s32[64,128]{1,0:T(8,128)S(1)}, s32[64,128]{1,0:T(8,128)S(1)}, u32[]{:S(2)}, u32[]{:S(2)}) collective-permute-start(s32[64,128]{1,0:T(8,128)S(1)} %dynamic-slice_add_fusion.2), channel_id=1, source_target_pairs={{0,16},{1,17},{2,18},{3,19},{4,20},{5,21},{6,22},{7,23},{8,24},{9,... | collective-permute-start | bytes 98312 | tf_op jit(solution)/shard_map/ppermute | solution.py:28
  41.6 4.8 %collective-permute-start.9 = (s32[64,128]{1,0:T(8,128)S(1)}, s32[64,128]{1,0:T(8,128)S(1)}, u32[]{:S(2)}, u32[]{:S(2)}) collective-permute-start(s32[64,128]{1,0:T(8,128)S(1)} %dynamic-slice_add_fusion.2), channel_id=1, source_target_pairs={{0,8},{1,9},{2,10},{3,11},{4,12},{5,13},{6,14},{7,15},{8,0},{9,1},... | collective-permute-start | bytes 98312 | tf_op jit(solution)/shard_map/ppermute | solution.py:28
  43.1 41.5 %collective-permute-start.23 = (bf16[1536,512]{1,0:T(8,128)(2,1)}, bf16[1536,512]{1,0:T(8,128)(2,1)S(1)}, u32[]{:S(2)}, u32[]{:S(2)}) collective-permute-start(bf16[1536,512]{1,0:T(8,128)(2,1)} %get-tuple-element.105), channel_id=1, source_target_pairs={{0,2},{1,3},{2,0},{3,1},{4,6},{5,7},{6,4},{7,5},{8,10},{9,11},{10,... | collective-permute-start | bytes 4718600 | tf_op jit(solution)/shard_map/ppermute | solution.py:28
  54.7 9.9 %collective-permute-start.16 = (bf16[512,512]{1,0:T(8,128)(2,1)}, bf16[512,512]{1,0:T(8,128)(2,1)}, u32[]{:S(2)}, u32[]{:S(2)}) collective-permute-start(bf16[512,512]{1,0:T(8,128)(2,1)} %get-tuple-element.82), channel_id=1, source_target_pairs={{0,1},{1,0},{2,3},{3,2},{4,5},{5,4},{6,7},{7,6},{8,9},{9,8},{10,11... | collective-permute-start | bytes 1572872 | tf_op jit(solution)/shard_map/ppermute | solution.py:28
  54.7 6.0 %collective-permute-start.15 = (s32[64,128]{1,0:T(8,128)S(1)}, s32[64,128]{1,0:T(8,128)S(1)}, u32[]{:S(2)}, u32[]{:S(2)}) collective-permute-start(s32[64,128]{1,0:T(8,128)S(1)} %add_add_fusion.1), channel_id=1, source_target_pairs={{0,96},{1,97},{2,98},{3,99},{4,100},{5,101},{6,102},{7,103},{8,104... | collective-permute-start | bytes 98312 | tf_op jit(solution)/shard_map/ppermute | solution.py:28
  56.6 5.1 %collective-permute-start.14 = (s32[64,128]{1,0:T(8,128)S(1)}, s32[64,128]{1,0:T(8,128)S(1)}, u32[]{:S(2)}, u32[]{:S(2)}) collective-permute-start(s32[64,128]{1,0:T(8,128)S(1)} %add_add_fusion.1), channel_id=1, source_target_pairs={{0,64},{1,65},{2,66},{3,67},{4,68},{5,69},{6,70},{7,71},{8,72},{9,... | collective-permute-start | bytes 98312 | tf_op jit(solution)/shard_map/ppermute | solution.py:28
  60.6 3.9 %collective-permute-start.13 = (s32[64,128]{1,0:T(8,128)S(1)}, s32[64,128]{1,0:T(8,128)S(1)}, u32[]{:S(2)}, u32[]{:S(2)}) collective-permute-start(s32[64,128]{1,0:T(8,128)S(1)} %add_add_fusion.1), channel_id=1, source_target_pairs={{0,32},{1,33},{2,34},{3,35},{4,36},{5,37},{6,38},{7,39},{8,40},{9,... | collective-permute-start | bytes 98312 | tf_op jit(solution)/shard_map/ppermute | solution.py:28
  61.7 8.1 %collective-permute-start.17 = (bf16[512,512]{1,0:T(8,128)(2,1)}, bf16[512,512]{1,0:T(8,128)(2,1)}, u32[]{:S(2)}, u32[]{:S(2)}) collective-permute-start(bf16[512,512]{1,0:T(8,128)(2,1)} %get-tuple-element.83), channel_id=1, source_target_pairs={{0,1},{1,0},{2,3},{3,2},{4,5},{5,4},{6,7},{7,6},{8,9},{9,8},{10,11... | collective-permute-start | bytes 1572872 | tf_op jit(solution)/shard_map/ppermute | solution.py:28
  64.6 5.2 %collective-permute-start.18 = (bf16[512,512]{1,0:T(8,128)(2,1)}, bf16[512,512]{1,0:T(8,128)(2,1)}, u32[]{:S(2)}, u32[]{:S(2)}) collective-permute-start(bf16[512,512]{1,0:T(8,128)(2,1)} %get-tuple-element.84), channel_id=1, source_target_pairs={{0,1},{1,0},{2,3},{3,2},{4,5},{5,4},{6,7},{7,6},{8,9},{9,8},{10,11... | collective-permute-start | bytes 1572872 | tf_op jit(solution)/shard_map/ppermute | solution.py:28
  64.6 5.2 %collective-permute-start.19 = (bf16[512,512]{1,0:T(8,128)(2,1)}, bf16[512,512]{1,0:T(8,128)(2,1)}, u32[]{:S(2)}, u32[]{:S(2)}) collective-permute-start(bf16[512,512]{1,0:T(8,128)(2,1)} %get-tuple-element.85), channel_id=1, source_target_pairs={{0,1},{1,0},{2,3},{3,2},{4,5},{5,4},{6,7},{7,6},{8,9},{9,8},{10,11... | collective-permute-start | bytes 1572872 | tf_op jit(solution)/shard_map/ppermute | solution.py:28
  69.8 12.1 %collective-permute-start.20 = (s32[256,128]{1,0:T(8,128)S(1)}, s32[256,128]{1,0:T(8,128)S(1)}, u32[]{:S(2)}, u32[]{:S(2)}) collective-permute-start(s32[256,128]{1,0:T(8,128)S(1)} %add_select_fusion.4), channel_id=1, source_target_pairs={{0,128},{1,129},{2,130},{3,131},{4,132},{5,133},{6,134},{7,135},{8... | collective-permute-start | bytes 393224 | tf_op jit(solution)/shard_map/ppermute | solution.py:28
  69.9 24.7 %collective-permute-start.22 = (bf16[512,512]{1,0:T(8,128)(2,1)}, bf16[512,512]{1,0:T(8,128)(2,1)S(1)}, u32[]{:S(2)}, u32[]{:S(2)}) collective-permute-start(bf16[512,512]{1,0:T(8,128)(2,1)} %get-tuple-element.102), channel_id=1, source_target_pairs={{0,2},{1,3},{2,0},{3,1},{4,6},{5,7},{6,4},{7,5},{8,10},{9,11},{10,... | collective-permute-start | bytes 1572872 | tf_op jit(solution)/shard_map/ppermute | solution.py:28
  70.5 14.0 %copy-start = (f32[1536,512]{1,0:T(8,128)S(1)}, f32[1536,512]{1,0:T(8,128)}, u32[]{:S(2)}) copy-start(f32[1536,512]{1,0:T(8,128)} %get-tuple-element.103.own_ref) | copy-start | bytes 9437188
  81.9 4.5 %copy-start.2 = (f32[1536,128]{1,0:T(8,128)S(1)}, f32[1536,128]{1,0:T(8,128)}, u32[]{:S(2)}) copy-start(f32[1536,128]{1,0:T(8,128)} %param.15) | copy-start | bytes 2359300
  81.9 4.5 %copy-start.5 = (f32[1536,128]{1,0:T(8,128)S(1)}, f32[1536,128]{1,0:T(8,128)}, u32[]{:S(2)}) copy-start(f32[1536,128]{1,0:T(8,128)} %param.17) | copy-start | bytes 2359300
  86.4 8.3 %copy-start.1 = (f32[512,512]{1,0:T(8,128)S(1)}, f32[512,512]{1,0:T(8,128)}, u32[]{:S(2)}) copy-start(f32[512,512]{1,0:T(8,128)} %get-tuple-element.101.own_ref) | copy-start | bytes 3145732
  (2 other events, 4.4 us)

commit v3 on v2

--- a/solution.py
+++ b/solution.py
@@ -160,13 +160,12 @@
 pieces = 4
 
 
-def token_kernel(me_ref, near_hbm, *refs):
-    far_hbm = refs[:4]
-    whole_hbm = refs[4:7]
-    piece_hbm = refs[7 : 7 + pieces]
-    x_hbm, gain_ref, cot_ref, inv_ref, keys_ref, out_hbm = refs[7 + pieces : 13 + pieces]
-    near, far, w, x, out, sems, out_sems = refs[13 + pieces :]
-    _, tokens, slab = near.shape
+def token_kernel(me_ref, *refs):
+    whole_hbm = refs[:3]
+    piece_hbm = refs[3 : 3 + pieces]
+    x_hbm, gain_ref, cot_ref, inv_ref, keys_ref, out_hbm = refs[3 + pieces : 9 + pieces]
+    w, x, out, sems, out_sems = refs[9 + pieces :]
+    _, tokens, slab = x.shape
     half = slab // 2
     width = 4 * slab
     me = me_ref[0]
@@ -181,41 +180,35 @@
     def column(s, h):
         return pl.multiple_of((me ^ s) * slab + h * half, half)
 
-    waits = []
+    x_waits = []
+    w_waits = []
     for s in range(4):
-        group = []
-        if s % 2 == 0:
-            group.append(load(near_hbm.at[s // 2], near.at[s // 2]))
-        else:
-            for k in (s - 1, s):
-                group.append(load(far_hbm[k], far.at[k]))
+        x_waits.append(load(x_hbm.at[:, pl.ds(column(s, 0), slab)], x.at[s]))
         if s < 3:
-            group.append(load(whole_hbm[s], w.at[s]))
+            w_waits.append([load(whole_hbm[s], w.at[s])])
         else:
             rows = slab // pieces
-            for k in range(pieces):
-                group.append(load(piece_hbm[k], w.at[s, pl.ds(k * rows, rows)]))
-        waits.append(group)
-    x_waits = [load(x_hbm.at[:, pl.ds(column(s, 0), slab)], x.at[s]) for s in range(4)]
-
+            w_waits.append(
+                [load(piece_hbm[k], w.at[s, pl.ds(k * rows, rows)]) for k in range(pieces)]
+            )
+
+    inv = inv_ref[:, :1]
     keys = jnp.zeros(keys_ref.shape, f32)
     for s in range(4):
-        for copy in waits[s]:
+        x_waits[s].wait()
+        for copy in w_waits[s]:
             copy.wait()
-        if s % 2 == 0:
-            keys = keys + jnp.dot(near[s // 2], w[s], preferred_element_type=f32)
-        else:
-            for h in range(2):
-                part = w[s, h * half : (h + 1) * half, :]
-                keys = keys + jnp.dot(far[s - 1 + h], part, preferred_element_type=f32)
+        for h in range(2):
+            values = x[s, :, h * half : (h + 1) * half].astype(f32)
+            normed = (values * inv * gain_ref[:, pl.ds(column(s, h), half)]).astype(bf16)
+            part = w[s, h * half : (h + 1) * half, :]
+            keys = keys + jnp.dot(normed, part, preferred_element_type=f32)
     keys_ref[...] = keys.astype(bf16)
     cot = cot_ref[...]
-    inv = inv_ref[:, :1]
     factor = inv * inv * (jnp.sum(cot.astype(f32) * keys, axis=1, keepdims=True) / width)
 
     sent = []
     for s in range(4):
-        x_waits[s].wait()
         for h in range(2):
             part = w[s, h * half : (h + 1) * half, :]
             dnormed = lax.dot_general(cot, part, (((1,), (1,)), ((), ())), preferred_element_type=f32)
@@ -231,58 +224,31 @@
         copy.wait()
 
 
-def token_outputs(me, near, far, whole, parts, hidden, gain, cot, inv):
+def token_outputs(me, whole, parts, hidden, gain, cot, inv):
     tokens, width = hidden.shape
     slab = width // 4
     keys_width = cot.shape[1]
     far_off = pl.BlockSpec(memory_space=pl.ANY)
     close = pl.BlockSpec(memory_space=pltpu.VMEM)
-    loads = 2 + 4 + 3 + pieces + 4
     return pl.pallas_call(
         token_kernel,
-        in_specs=[pl.BlockSpec(memory_space=pltpu.SMEM)] + [far_off] * (9 + pieces) + [close] * 3,
+        in_specs=[pl.BlockSpec(memory_space=pltpu.SMEM)] + [far_off] * (4 + pieces) + [close] * 3,
         out_specs=[close, far_off],
         out_shape=[
             jax.ShapeDtypeStruct((tokens, keys_width), bf16),
             jax.ShapeDtypeStruct((tokens, width), bf16),
         ],
         scratch_shapes=[
-            pltpu.VMEM((2, tokens, slab), bf16),
-            pltpu.VMEM((4, tokens, slab // 2), bf16),
             pltpu.VMEM((4, slab, keys_width), bf16),
             pltpu.VMEM((4, tokens, slab), bf16),
             pltpu.VMEM((4, 2, tokens, slab // 2), bf16),
-            pltpu.SemaphoreType.DMA((loads,)),
+            pltpu.SemaphoreType.DMA((7 + pieces,)),
             pltpu.SemaphoreType.DMA((8,)),
         ],
         compiler_params=params(),
         cost_estimate=small,
         name="keys_and_input_grad",
-    )(me, near, *far, *whole, *parts, hidden, gain, cot, inv)
-
-
-def split_kernel(source, *targets):
-    rows = targets[0].shape[0]
-    for k, target in enumerate(targets):
-
-        @pl.when(pl.program_id(0) == k)
-        def _(target=target):
-            target[...] = source[...]
-
-
-def in_pieces(value):
-    rows, width = value.shape
-    rows = rows // pieces
-    return pl.pallas_call(
-        split_kernel,
-        grid=(pieces,),
-        in_specs=[pl.BlockSpec((rows, width), lambda i: (i, 0))],
-        out_specs=[pl.BlockSpec((rows, width), lambda i: (0, 0))] * pieces,
-        out_shape=[pltpu.HBM((rows, width), value.dtype)] * pieces,
-        compiler_params=params(),
-        cost_estimate=small,
-        name="split",
-    )(value)
+    )(me, *whole, *parts, hidden, gain, cot, inv)
 
 
 def packed_codes(global_base, replica_params, level, dither_seeds, fragment_index):
@@ -309,9 +275,20 @@
     return kept + got, done
 
 
-def exchange(total, masks, work):
-    got, done = beside([send(total, mask) for mask in masks], work())
-    return sum(got, total), done
+def exchange(total, mask, work):
+    got, done = beside(send(total, mask), work())
+    return total + got, done
+
+
+def scatter_y(total, work):
+    y = (lax.axis_index("rep") // 2) % 4
+    quarter = total.shape[0] // 4
+
+    def part(k):
+        return lax.dynamic_slice_in_dim(total, (y ^ k) * quarter, quarter, 0)
+
+    got, done = beside([send(part(k), y_bit * k) for k in (1, 2, 3)], work())
+    return sum(got, part(0)), done
 
 
 def in_order(low, mine, other):
@@ -320,16 +297,14 @@
     )
 
 
-def rejoin_four(total, work):
-    z = lax.axis_index("rep") // 8
-    got, done = beside([send(total, z_bit * step) for step in (1, 2, 3)], work())
-    even = z % 2 == 0
-    near_pair = in_order(even, total, got[0])
-    far_pair = in_order(even, got[1], got[2])
-    return in_order((z // 2) % 2 == 0, near_pair, far_pair), done
-
-
-def rejoin(total, step, work):
+def gather_y(total, work):
+    y = (lax.axis_index("rep") // 2) % 4
+    got, done = beside([send(total, y_bit * k) for k in (1, 2, 3)], work())
+    even = y % 2 == 0
+    return in_order(y < 2, in_order(even, total, got[0]), in_order(even, got[1], got[2])), done
+
+
+def gather_z(total, step, work):
     z = lax.axis_index("rep") // 8
     other, done = beside(send(total, z_bit * step), work())
     return in_order((z // step) % 2 == 0, total, other), done
@@ -372,31 +347,32 @@
     total, hidden = lax.optimization_barrier((total, hidden_in))
     total, (near, far, inv) = halve(total, 4, lambda: norm_slabs(me, hidden, gain))
     total, came = halve(total, 2, lambda: [send(part, core_bit) for part in far])
-    total, out_rows = exchange(
+    total, out_rows = scatter_y(
+        total, lambda: grad_rows(near, came, key_cot, cot_sibling, 1, bf16, "grad_out")
+    )
+    in_rows = [send(rows, x_lo_bit) for rows in out_rows]
+    total, own_rows = exchange(
         total,
-        (x_hi_bit | z_bit,),
-        lambda: grad_rows(near, came, key_cot, cot_sibling, 1, bf16, "grad_out"),
-    )
-    in_rows = [send(rows, x_lo_bit) for rows in out_rows]
-    total, _ = halve(total, 1, nothing)
-    total, _ = exchange(total, (y_bit, y_bit * 2, y_bit * 3), nothing)
+        x_hi_bit | z_bit,
+        lambda: grad_rows(near, came, key_cot, cot_sibling, 0, f32, "grad_own"),
+    )
+    total, _ = exchange(total, z_bit, nothing)
     total, partner = lax.optimization_barrier((total, partner))
-    diagonal = [send(part, core_bit) for part in in_pieces(partner)]
-    total, (diagonal, own_rows) = rejoin_four(
-        total,
-        lambda: (diagonal, grad_rows(near, came, key_cot, cot_sibling, 0, f32, "grad_own")),
-    )
-    total, (keys, input_grad) = rejoin(
+    quarter = partner.shape[0] // pieces
+    diagonal = [send(partner[k * quarter : (k + 1) * quarter], core_bit) for k in range(pieces)]
+    total, _ = gather_y(total, nothing)
+    total, diagonal = gather_z(total, 2, lambda: diagonal)
+    total, (keys, input_grad) = gather_z(
         total,
         4,
         lambda: token_outputs(
-            me, near, far, (own, sibling, partner), diagonal, hidden, gain, key_cot, inv
+            me, (own, sibling, partner), diagonal, hidden, gain, key_cot, inv
         ),
     )
+    input_grad, in_rows[0] = lax.optimization_barrier((input_grad, in_rows[0]))
     new_base, new_momentum = outer_update(
         total, global_base, outer_momentum, level, lax.axis_size("rep")
     )
-    input_grad, in_rows[0] = lax.optimization_barrier((input_grad, in_rows[0]))
     weight_grad = None
     for first, own_part, in_part in zip(cuts, own_rows, in_rows):
         weight_grad = add_rows(own_part, in_part, first, weight_grad)

time: 95.9 us -> 94.9 us (0.990)
  Pallas kernels: 32.4 us -> 27.6 us
  starting transfers between devices: 18.2 us -> 21.4 us
  local copies, waits for them, and re-layouts: 0.78 us -> 3.2 us
  waiting for transfers between devices: 36.2 us -> 34.2 us
    pallas_call x1 -> x0, Pallas kernels: 3.7 us -> none  [in_pieces(): pl.pallas_call(split_kernel, grid=(pieces,), in_specs=[pl.BlockSpec((rows...]
    ppermute x24 -> x25, starting transfers between devices: 18.2 us -> 21.4 us  [send(): return lax.ppermute(value, axes, flip(bit))]
    slice x0 -> x1, local copies, waits for them, and re-layouts: none -> 2.86 us  [per_device(): partner[k * quarter:(k + 1) * quarter]]
    ppermute x24 -> x25, waiting for transfers between devices: 36.2 us -> 34.2 us  [send(): return lax.ppermute(value, axes, flip(bit))]
    pallas_call x1, Pallas kernels: 11.4 us -> 10.3 us  [token_outputs(): pl.pallas_call(token_kernel, in_specs=[pl.BlockSpec(memory_space=pltpu.SM...]
  transfers between devices with their start and end apart: 24 -> 25, of which waited for: 12 -> 13; matrix products, arithmetic and copies ran while one was open for 7% -> 10% of each run, Pallas kernels for 33% -> 28%
where the time goes in v3:
time: 94.9 us; the launch traced here: 94.5 us
  waiting for transfers between devices  34.2 us (36%)
  Pallas kernels  27.6 us (29%)
  starting transfers between devices  21.4 us (23%)
  other arithmetic  6.56 us (7%)
  local copies, waits for them, and re-layouts  3.2 us (3%)
  between operations  1.58 us (2%)
    ppermute x25, waiting for transfers between devices, send(): return lax.ppermute(value, axes, flip(bit))  34.2 us
    ppermute x25, starting transfers between devices, send(): return lax.ppermute(value, axes, flip(bit))  21.4 us
    pallas_call x1, Pallas kernels, token_outputs(): pl.pallas_call(token_kernel, in_specs=[pl.BlockSpec(memory_space=pltpu.SM...  10.3 us
    pallas_call x2, Pallas kernels, grad_rows(): pl.pallas_call(grad_kernel, grid=(1,), in_specs=[pl.BlockSpec((1, tokens,...  8.74 us
    pallas_call x1, Pallas kernels, norm_slabs(): pl.pallas_call(norm_kernel, grid_spec=pltpu.PrefetchScalarGridSpec(num_sc...  5.87 us
    add x1, other arithmetic, packed_codes(): shifted = code + 8  3.39 us
    slice x1, local copies, waits for them, and re-layouts, per_device(): partner[k * quarter:(k + 1) * quarter]  2.86 us
    pallas_call x2, Pallas kernels, add_rows(): pl.pallas_call(add_kernel, grid=(rows // block,), in_specs=[part, part] +...  2.67 us
  transfers between devices with their start and end apart: 25, of which 13 were waited for; matrix products, arithmetic and copies ran while one was open for 10% of the time, Pallas kernels for 28%

profile of v3, /device:TPU:130, one launch (start us, length us, event | category | flops | bytes accessed | tf_op | source)
XLA Modules:
  0.0 94.5 jit_solution(15229331384435533334)
XLA Ops:
  0.6 0.6 collective-permute-start.12
  1.9 0.7 reduce
  2.6 0.8 select_reduce_fusion
  3.4 3.4 %fusion.10 = s32[1536,128]{1,0:T(8,128)S(1)} fusion(f32[1536,128]{1,0:T(8,128)} %param.15, bf16[1,1536,128]{2,1,0:T(8,128)(2,1)} %param.16, s32[]{:T(128)} %bitcast.1, s32[128]{0:T(128)S(1)} %iota_multiply_fusion, s32[1536]{0:T(1024)S(1)} %reduce, f32[1536]{0:T(1024)S(1)} %select_reduce_fusion), kind=kLoop, calls=%fused_computation.16 | loop fusion | flops 7667712 | bytes 1978884 | tf_op jit(solution)/shard_map/add | solution.py:260
  7.5 5.9 %norm.1 = (bf16[2,256,2048]{2,1,0:T(8,128)(2,1)}, bf16[256,1024]{1,0:T(8,128)(2,1)}, bf16[256,1024]{1,0:T(8,128)(2,1)}, bf16[256,1024]{1,0:T(8,128)(2,1)}, bf16[...) custom-call(s32[1]{0:T(128)} %bitcast.2.me_ref, bf16[256,8192]{1,0:T(8,128)(2,1)} %refs_7_, f32[1,8192]{1,0:T(1,128)} %bitcast.7), custom_call_target="tpu_custom_call" | custom-call | flops 1024 | bytes 1024 | tf_op jit(solution)/shard_map/norm/pallas_call | solution.py:78
  13.4 4.6 %collective-permute-done = s32[256,128]{1,0:T(8,128)S(1)} collective-permute-done((s32[256,128]{1,0:T(8,128)S(1)}, s32[256,128]{1,0:T(8,128)S(1)}, u32[]{:S(2)}, u32[]{:S(2)}) %collective-permute-start) | collective-permute-done | bytes 131104 | tf_op jit(solution)/shard_map/ppermute | solution.py:28
  18.1 2.2 %collective-permute-start.1 = (s32[128,128]{1,0:T(8,128)S(1)}, s32[128,128]{1,0:T(8,128)S(1)}, u32[]{:S(2)}, u32[]{:S(2)}) collective-permute-start(s32[128,128]{1,0:T(8,128)S(1)} %constant_dynamic-slice_fusion.3), channel_id=1, source_target_pairs={{0,64},{1,65},{2,66},{3,67},{4,68},{5,69},{6,70},{7,71},{8,72},{9,... | collective-permute-start | bytes 196616 | tf_op jit(solution)/shard_map/ppermute | solution.py:28
  20.8 2.6 %collective-permute-done.1 = s32[128,128]{1,0:T(8,128)S(1)} collective-permute-done((s32[128,128]{1,0:T(8,128)S(1)}, s32[128,128]{1,0:T(8,128)S(1)}, u32[]{:S(2)}, u32[]{:S(2)}) %collective-permute-start.1) | collective-permute-done | bytes 65568 | tf_op jit(solution)/shard_map/ppermute | solution.py:28
  24.0 1.4 %collective-permute-done.5.high_ref = bf16[256,1024]{1,0:T(8,128)(2,1)S(1)} collective-permute-done((bf16[256,1024]{1,0:T(8,128)(2,1)}, bf16[256,1024]{1,0:T(8,128)(2,1)S(1)}, u32[]{:S(2)}, u32[]{:S(2)}) %collective-permute-start.5) | collective-permute-done | bytes 524320 | tf_op jit(solution)/shard_map/ppermute | solution.py:28
  25.5 3.1 %collective-permute-start.8 = (s32[32,128]{1,0:T(8,128)S(1)}, s32[32,128]{1,0:T(8,128)S(1)}, u32[]{:S(2)}, u32[]{:S(2)}) collective-permute-start(s32[32,128]{1,0:T(8,128)S(1)} %get-tuple-element.112), channel_id=1, source_target_pairs={{0,24},{1,25},{2,26},{3,27},{4,28},{5,29},{6,30},{7,31},{8,16},{9,... | collective-permute-start | bytes 49160 | tf_op jit(solution)/shard_map/ppermute | solution.py:28
  28.6 0.6 collective-permute-start.7
  29.9 4.1 %grad_out.1 = (bf16[1536,512]{1,0:T(8,128)(2,1)}, bf16[512,512]{1,0:T(8,128)(2,1)}) custom-call(bf16[2,256,2048]{2,1,0:T(8,128)(2,1)} %get-tuple-element.68.mine_ref, bf16[256,1024]{1,0:T(8,128)(2,1)} %copy-done.8, bf16[256,1024]{1,0:T(8,128)(2,1)} %copy-done.9, bf16[256,512]{1,0:T(8,128)(2,1)} %refs_9_.1, bf16[256,512]{1,0:T(8,128)(2,1)} %copy-done.4), custom_call_target="tpu_custom_call" | custom-call | flops 1024 | bytes 1024 | tf_op jit(solution)/shard_map/grad_out/pallas_call | solution.py:120
  34.1 3.6 %collective-permute-start.10 = (s32[32,128]{1,0:T(8,128)S(1)}, s32[32,128]{1,0:T(8,128)S(1)}, u32[]{:S(2)}, u32[]{:S(2)}) collective-permute-start(s32[32,128]{1,0:T(8,128)S(1)} %add_add_fusion.1), channel_id=1, source_target_pairs={{0,36},{1,37},{2,38},{3,39},{4,32},{5,33},{6,34},{7,35},{8,44},{9,... | collective-permute-start | bytes 49160 | tf_op jit(solution)/shard_map/ppermute | solution.py:28
  37.7 4.6 %grad_own.1 = (f32[1536,512]{1,0:T(8,128)}, f32[512,512]{1,0:T(8,128)}) custom-call(bf16[2,256,2048]{2,1,0:T(8,128)(2,1)} %get-tuple-element.68.mine_ref, bf16[256,1024]{1,0:T(8,128)(2,1)} %copy-done.6, bf16[256,1024]{1,0:T(8,128)(2,1)} %copy-done.7, bf16[256,512]{1,0:T(8,128)(2,1)} %refs_9_.1, bf16[256,512]{1,0:T(8,128)(2,1)} %copy-done.4), custom_call_target="tpu_custom_call" | custom-call | flops 1024 | bytes 1024 | tf_op jit(solution)/shard_map/grad_own/pallas_call | solution.py:120
  42.8 1.8 %collective-permute-start.24 = (bf16[1536,512]{1,0:T(8,128)(2,1)}, bf16[1536,512]{1,0:T(8,128)(2,1)S(1)}, u32[]{:S(2)}, u32[]{:S(2)}) collective-permute-start(bf16[1536,512]{1,0:T(8,128)(2,1)} %get-tuple-element.99), channel_id=1, source_target_pairs={{0,2},{1,3},{2,0},{3,1},{4,6},{5,7},{6,4},{7,5},{8,10},{9,11},{10,... | collective-permute-start | bytes 4718600 | tf_op jit(solution)/shard_map/ppermute | solution.py:28
  44.6 1.6 %collective-permute-done.11 = s32[32,128]{1,0:T(8,128)S(1)} collective-permute-done((s32[32,128]{1,0:T(8,128)S(1)}, s32[32,128]{1,0:T(8,128)S(1)}, u32[]{:S(2)}, u32[]{:S(2)}) %collective-permute-start.11) | collective-permute-done | bytes 16416 | tf_op jit(solution)/shard_map/ppermute | solution.py:28
  46.2 3.7 %collective-permute-done.12.refs_2_ = bf16[2048,512]{1,0:T(8,128)(2,1)} collective-permute-done((bf16[2048,512]{1,0:T(8,128)(2,1)}, bf16[2048,512]{1,0:T(8,128)(2,1)}, u32[]{:S(2)}, u32[]{:S(2)}) %collective-permute-start.12) | collective-permute-done | bytes 2097184 | tf_op jit(solution)/shard_map/ppermute | solution.py:28
  49.9 2.9 %fusion.19 = (bf16[512,512]{1,0:T(8,128)(2,1)}, bf16[512,512]{1,0:T(8,128)(2,1)}, bf16[512,512]{1,0:T(8,128)(2,1)}, bf16[512,512]{1,0:T(8,128)(2,1)}) fusion(bf16[2048,512]{1,0:T(8,128)(2,1)} %collective-permute-done.12.refs_2_), kind=kLoop, calls=%fused_computation.52 | loop fusion | bytes 4194304 | tf_op jit(solution)/shard_map/slice | solution.py:362
  52.8 3.0 %collective-permute-start.15 = (s32[32,128]{1,0:T(8,128)S(1)}, s32[32,128]{1,0:T(8,128)S(1)}, u32[]{:S(2)}, u32[]{:S(2)}) collective-permute-start(s32[32,128]{1,0:T(8,128)S(1)} %add.185), channel_id=1, source_target_pairs={{0,24},{1,25},{2,26},{3,27},{4,28},{5,29},{6,30},{7,31},{8,16},{9,... | collective-permute-start | bytes 49160 | tf_op jit(solution)/shard_map/ppermute | solution.py:28
  55.8 0.6 collective-permute-start.14
  56.4 1.3 %collective-permute-done.15 = s32[32,128]{1,0:T(8,128)S(1)} collective-permute-done((s32[32,128]{1,0:T(8,128)S(1)}, s32[32,128]{1,0:T(8,128)S(1)}, u32[]{:S(2)}, u32[]{:S(2)}) %collective-permute-start.15) | collective-permute-done | bytes 16416 | tf_op jit(solution)/shard_map/ppermute | solution.py:28
  58.1 2.9 %collective-permute-done.14 = s32[32,128]{1,0:T(8,128)S(1)} collective-permute-done((s32[32,128]{1,0:T(8,128)S(1)}, s32[32,128]{1,0:T(8,128)S(1)}, u32[]{:S(2)}, u32[]{:S(2)}) %collective-permute-start.14) | collective-permute-done | bytes 16416 | tf_op jit(solution)/shard_map/ppermute | solution.py:28
  61.5 1.6 %collective-permute-start.16 = (s32[128,128]{1,0:T(8,128)S(1)}, s32[128,128]{1,0:T(8,128)S(1)}, u32[]{:S(2)}, u32[]{:S(2)}) collective-permute-start(s32[128,128]{1,0:T(8,128)S(1)} %add_select_fusion.5), channel_id=1, source_target_pairs={{0,64},{1,65},{2,66},{3,67},{4,68},{5,69},{6,70},{7,71},{8,72},{9,... | collective-permute-start | bytes 196616 | tf_op jit(solution)/shard_map/ppermute | solution.py:28
  63.0 4.4 %collective-permute-done.16 = s32[128,128]{1,0:T(8,128)S(1)} collective-permute-done((s32[128,128]{1,0:T(8,128)S(1)}, s32[128,128]{1,0:T(8,128)S(1)}, u32[]{:S(2)}, u32[]{:S(2)}) %collective-permute-start.16) | collective-permute-done | bytes 65568 | tf_op jit(solution)/shard_map/ppermute | solution.py:28
  68.0 1.7 %collective-permute-done.18.refs_4_ = bf16[512,512]{1,0:T(8,128)(2,1)} collective-permute-done((bf16[512,512]{1,0:T(8,128)(2,1)}, bf16[512,512]{1,0:T(8,128)(2,1)}, u32[]{:S(2)}, u32[]{:S(2)}) %collective-permute-start.18) | collective-permute-done | bytes 524320 | tf_op jit(solution)/shard_map/ppermute | solution.py:28
  69.7 0.7 collective-permute-done.17.refs_3_
  71.2 10.3 %keys_and_input_grad.1 = (bf16[256,512]{1,0:T(8,128)(2,1)}, bf16[256,8192]{1,0:T(8,128)(2,1)}) custom-call(s32[1]{0:T(128)} %bitcast.2.me_ref, bf16[2048,512]{1,0:T(8,128)(2,1)} %bitcast.4.refs_0_, bf16[2048,512]{1,0:T(8,128)(2,1)} %collective-permute-done.22.refs_1_, bf16[2048,512]{1,0:T(8,128)(2,1)} %collective-permute-done.12.refs_2_, ...), custom_call_target="tpu_custom_call" | custom-call | flops 1024 | bytes 1024 | tf_op jit(solution)/shard_map/keys_and_input_grad/pallas_call | solution.py:233
  81.6 1.9 %collective-permute-done.24.came_ref = bf16[1536,512]{1,0:T(8,128)(2,1)S(1)} collective-permute-done((bf16[1536,512]{1,0:T(8,128)(2,1)}, bf16[1536,512]{1,0:T(8,128)(2,1)S(1)}, u32[]{:S(2)}, u32[]{:S(2)}) %collective-permute-start.24) | collective-permute-done | bytes 1572896 | tf_op jit(solution)/shard_map/ppermute | solution.py:28
  83.5 1.8 %add.354.refs_0_ = bf16[1,2048,512]{2,1,0:T(8,128)(2,1)} custom-call(f32[1536,512]{1,0:T(8,128)S(1)} %copy-done, bf16[1536,512]{1,0:T(8,128)(2,1)S(1)} %collective-permute-done.24.came_ref), custom_call_target="tpu_custom_call" | custom-call | flops 1024 | bytes 1024 | tf_op jit(solution)/shard_map/add/pallas_call | solution.py:147
  85.4 1.5 %multiply_subtract_fusion = (f32[1536,128]{1,0:T(8,128)}, f32[1536,128]{1,0:T(8,128)}) fusion(f32[1536,128]{1,0:T(8,128)S(1)} %copy-done.2, s32[512,128]{1,0:T(8,128)S(1)} %get-tuple-element.111, s32[512,128]{1,0:T(8,128)S(1)} %get-tuple-element.110, s32[512,128]{1,0:T(8,128)S(1)} %get-tuple-element.109, f32[1536]{0:T(1024)S(1)} %divide_multiply_fusion, ...), kind=kLoop, calls=%fused_computation.22 | loop fusion | flops 2162688 | bytes 3938304 | tf_op jit(solution)/shard_map/sub | solution.py:321
  86.8 6.8 %collective-permute-done.23.came_ref = bf16[512,512]{1,0:T(8,128)(2,1)S(1)} collective-permute-done((bf16[512,512]{1,0:T(8,128)(2,1)}, bf16[512,512]{1,0:T(8,128)(2,1)S(1)}, u32[]{:S(2)}, u32[]{:S(2)}) %collective-permute-start.23) | collective-permute-done | bytes 524320 | tf_op jit(solution)/shard_map/ppermute | solution.py:28
  93.6 0.9 add.355
  (69 shorter events, 5.2 us)
Async XLA Ops:
  0.6 49.3 %collective-permute-start.12 = (bf16[2048,512]{1,0:T(8,128)(2,1)}, bf16[2048,512]{1,0:T(8,128)(2,1)}, u32[]{:S(2)}, u32[]{:S(2)}) collective-permute-start(bf16[2048,512]{1,0:T(8,128)(2,1)} %bitcast.4.refs_0_), channel_id=1, source_target_pairs={{0,2},{1,3},{2,0},{3,1},{4,6},{5,7},{6,4},{7,5},{8,10},{9,11},{10,... | collective-permute-start | bytes 6291464 | tf_op jit(solution)/shard_map/ppermute | solution.py:28
  7.0 11.1 %collective-permute-start = (s32[256,128]{1,0:T(8,128)S(1)}, s32[256,128]{1,0:T(8,128)S(1)}, u32[]{:S(2)}, u32[]{:S(2)}) collective-permute-start(s32[256,128]{1,0:T(8,128)S(1)} %constant_dynamic-slice_fusion.4), channel_id=1, source_target_pairs={{0,128},{1,129},{2,130},{3,131},{4,132},{5,133},{6,134},{7,135},{8... | collective-permute-start | bytes 393224 | tf_op jit(solution)/shard_map/ppermute | solution.py:28
  7.5 16.3 %copy-start.3 = (bf16[256,512]{1,0:T(8,128)(2,1)S(1)}, bf16[256,512]{1,0:T(8,128)(2,1)}, u32[]{:S(2)}) copy-start(bf16[256,512]{1,0:T(8,128)(2,1)} %refs_9_.1) | copy-start | bytes 786436
  18.1 5.3 %collective-permute-start.1 = (s32[128,128]{1,0:T(8,128)S(1)}, s32[128,128]{1,0:T(8,128)S(1)}, u32[]{:S(2)}, u32[]{:S(2)}) collective-permute-start(s32[128,128]{1,0:T(8,128)S(1)} %constant_dynamic-slice_fusion.3), channel_id=1, source_target_pairs={{0,64},{1,65},{2,66},{3,67},{4,68},{5,69},{6,70},{7,71},{8,72},{9,... | collective-permute-start | bytes 196616 | tf_op jit(solution)/shard_map/ppermute | solution.py:28
  20.3 3.1 %collective-permute-start.2 = (bf16[256,1024]{1,0:T(8,128)(2,1)}, bf16[256,1024]{1,0:T(8,128)(2,1)S(1)}, u32[]{:S(2)}, u32[]{:S(2)}) collective-permute-start(bf16[256,1024]{1,0:T(8,128)(2,1)} %get-tuple-element.63), channel_id=1, source_target_pairs={{0,1},{1,0},{2,3},{3,2},{4,5},{5,4},{6,7},{7,6},{8,9},{9,8},{10,11... | collective-permute-start | bytes 1572872 | tf_op jit(solution)/shard_map/ppermute | solution.py:28
  20.3 3.6 %collective-permute-start.3 = (bf16[256,1024]{1,0:T(8,128)(2,1)}, bf16[256,1024]{1,0:T(8,128)(2,1)S(1)}, u32[]{:S(2)}, u32[]{:S(2)}) collective-permute-start(bf16[256,1024]{1,0:T(8,128)(2,1)} %get-tuple-element.64), channel_id=1, source_target_pairs={{0,1},{1,0},{2,3},{3,2},{4,5},{5,4},{6,7},{7,6},{8,9},{9,8},{10,11... | collective-permute-start | bytes 1572872 | tf_op jit(solution)/shard_map/ppermute | solution.py:28
  20.8 3.3 %collective-permute-start.4 = (bf16[256,1024]{1,0:T(8,128)(2,1)}, bf16[256,1024]{1,0:T(8,128)(2,1)S(1)}, u32[]{:S(2)}, u32[]{:S(2)}) collective-permute-start(bf16[256,1024]{1,0:T(8,128)(2,1)} %get-tuple-element.65), channel_id=1, source_target_pairs={{0,1},{1,0},{2,3},{3,2},{4,5},{5,4},{6,7},{7,6},{8,9},{9,8},{10,11... | collective-permute-start | bytes 1572872 | tf_op jit(solution)/shard_map/ppermute | solution.py:28
  23.3 2.1 %collective-permute-start.5 = (bf16[256,1024]{1,0:T(8,128)(2,1)}, bf16[256,1024]{1,0:T(8,128)(2,1)S(1)}, u32[]{:S(2)}, u32[]{:S(2)}) collective-permute-start(bf16[256,1024]{1,0:T(8,128)(2,1)} %get-tuple-element.66), channel_id=1, source_target_pairs={{0,1},{1,0},{2,3},{3,2},{4,5},{5,4},{6,7},{7,6},{8,9},{9,8},{10,11... | collective-permute-start | bytes 1572872 | tf_op jit(solution)/shard_map/ppermute | solution.py:28
  23.3 14.4 %copy-start.6 = (bf16[256,1024]{1,0:T(8,128)(2,1)}, bf16[256,1024]{1,0:T(8,128)(2,1)S(1)}, u32[]{:S(2)}) copy-start(bf16[256,1024]{1,0:T(8,128)(2,1)S(1)} %collective-permute-done.2.low_ref) | copy-start | bytes 1572868
  23.4 47.9 %collective-permute-start.22 = (bf16[2048,512]{1,0:T(8,128)(2,1)}, bf16[2048,512]{1,0:T(8,128)(2,1)}, u32[]{:S(2)}, u32[]{:S(2)}) collective-permute-start(bf16[2048,512]{1,0:T(8,128)(2,1)} %bitcast.4.refs_0_), channel_id=1, source_target_pairs={{0,1},{1,0},{2,3},{3,2},{4,5},{5,4},{6,7},{7,6},{8,9},{9,8},{10,11... | collective-permute-start | bytes 6291464 | tf_op jit(solution)/shard_map/ppermute | solution.py:28
  23.9 13.9 %copy-start.7 = (bf16[256,1024]{1,0:T(8,128)(2,1)}, bf16[256,1024]{1,0:T(8,128)(2,1)S(1)}, u32[]{:S(2)}) copy-start(bf16[256,1024]{1,0:T(8,128)(2,1)S(1)} %collective-permute-done.3.high_ref) | copy-start | bytes 1572868
  23.9 5.4 %collective-permute-start.9 = (bf16[256,512]{1,0:T(8,128)(2,1)S(1)}, bf16[256,512]{1,0:T(8,128)(2,1)S(1)}, u32[]{:S(2)}, u32[]{:S(2)}) collective-permute-start(bf16[256,512]{1,0:T(8,128)(2,1)S(1)} %copy-done.3), channel_id=1, source_target_pairs={{0,1},{1,0},{2,3},{3,2},{4,5},{5,4},{6,7},{7,6},{8,9},{9,8},{10,11... | collective-permute-start | bytes 786440 | tf_op jit(solution)/shard_map/ppermute | solution.py:28
  24.0 5.6 %copy-start.8 = (bf16[256,1024]{1,0:T(8,128)(2,1)}, bf16[256,1024]{1,0:T(8,128)(2,1)S(1)}, u32[]{:S(2)}) copy-start(bf16[256,1024]{1,0:T(8,128)(2,1)S(1)} %collective-permute-done.4.low_ref) | copy-start | bytes 1572868
  25.5 4.2 %copy-start.9 = (bf16[256,1024]{1,0:T(8,128)(2,1)}, bf16[256,1024]{1,0:T(8,128)(2,1)S(1)}, u32[]{:S(2)}) copy-start(bf16[256,1024]{1,0:T(8,128)(2,1)S(1)} %collective-permute-done.5.high_ref) | copy-start | bytes 1572868
  25.5 8.5 %collective-permute-start.8 = (s32[32,128]{1,0:T(8,128)S(1)}, s32[32,128]{1,0:T(8,128)S(1)}, u32[]{:S(2)}, u32[]{:S(2)}) collective-permute-start(s32[32,128]{1,0:T(8,128)S(1)} %get-tuple-element.112), channel_id=1, source_target_pairs={{0,24},{1,25},{2,26},{3,27},{4,28},{5,29},{6,30},{7,31},{8,16},{9,... | collective-permute-start | bytes 49160 | tf_op jit(solution)/shard_map/ppermute | solution.py:28
  28.6 5.4 %collective-permute-start.7 = (s32[32,128]{1,0:T(8,128)S(1)}, s32[32,128]{1,0:T(8,128)S(1)}, u32[]{:S(2)}, u32[]{:S(2)}) collective-permute-start(s32[32,128]{1,0:T(8,128)S(1)} %get-tuple-element.113), channel_id=1, source_target_pairs={{0,16},{1,17},{2,18},{3,19},{4,20},{5,21},{6,22},{7,23},{8,24},{9,... | collective-permute-start | bytes 49160 | tf_op jit(solution)/shard_map/ppermute | solution.py:28
  29.2 4.8 %collective-permute-start.6 = (s32[32,128]{1,0:T(8,128)S(1)}, s32[32,128]{1,0:T(8,128)S(1)}, u32[]{:S(2)}, u32[]{:S(2)}) collective-permute-start(s32[32,128]{1,0:T(8,128)S(1)} %get-tuple-element.114), channel_id=1, source_target_pairs={{0,8},{1,9},{2,10},{3,11},{4,12},{5,13},{6,14},{7,15},{8,0},{9,1},... | collective-permute-start | bytes 49160 | tf_op jit(solution)/shard_map/ppermute | solution.py:28
  34.1 8.3 %collective-permute-start.10 = (s32[32,128]{1,0:T(8,128)S(1)}, s32[32,128]{1,0:T(8,128)S(1)}, u32[]{:S(2)}, u32[]{:S(2)}) collective-permute-start(s32[32,128]{1,0:T(8,128)S(1)} %add_add_fusion.1), channel_id=1, source_target_pairs={{0,36},{1,37},{2,38},{3,39},{4,32},{5,33},{6,34},{7,35},{8,44},{9,... | collective-permute-start | bytes 49160 | tf_op jit(solution)/shard_map/ppermute | solution.py:28
  42.4 3.8 %collective-permute-start.11 = (s32[32,128]{1,0:T(8,128)S(1)}, s32[32,128]{1,0:T(8,128)S(1)}, u32[]{:S(2)}, u32[]{:S(2)}) collective-permute-start(s32[32,128]{1,0:T(8,128)S(1)} %add.184), channel_id=1, source_target_pairs={{0,32},{1,33},{2,34},{3,35},{4,36},{5,37},{6,38},{7,39},{8,40},{9,... | collective-permute-start | bytes 49160 | tf_op jit(solution)/shard_map/ppermute | solution.py:28
  42.8 40.7 %collective-permute-start.24 = (bf16[1536,512]{1,0:T(8,128)(2,1)}, bf16[1536,512]{1,0:T(8,128)(2,1)S(1)}, u32[]{:S(2)}, u32[]{:S(2)}) collective-permute-start(bf16[1536,512]{1,0:T(8,128)(2,1)} %get-tuple-element.99), channel_id=1, source_target_pairs={{0,2},{1,3},{2,0},{3,1},{4,6},{5,7},{6,4},{7,5},{8,10},{9,11},{10,... | collective-permute-start | bytes 4718600 | tf_op jit(solution)/shard_map/ppermute | solution.py:28
  52.8 14.7 %collective-permute-start.20 = (bf16[512,512]{1,0:T(8,128)(2,1)}, bf16[512,512]{1,0:T(8,128)(2,1)S(1)}, u32[]{:S(2)}, u32[]{:S(2)}) collective-permute-start(bf16[512,512]{1,0:T(8,128)(2,1)} %get-tuple-element.105), channel_id=1, source_target_pairs={{0,1},{1,0},{2,3},{3,2},{4,5},{5,4},{6,7},{7,6},{8,9},{9,8},{10,11... | collective-permute-start | bytes 1572872 | tf_op jit(solution)/shard_map/ppermute | solution.py:28
  52.8 4.9 %collective-permute-start.15 = (s32[32,128]{1,0:T(8,128)S(1)}, s32[32,128]{1,0:T(8,128)S(1)}, u32[]{:S(2)}, u32[]{:S(2)}) collective-permute-start(s32[32,128]{1,0:T(8,128)S(1)} %add.185), channel_id=1, source_target_pairs={{0,24},{1,25},{2,26},{3,27},{4,28},{5,29},{6,30},{7,31},{8,16},{9,... | collective-permute-start | bytes 49160 | tf_op jit(solution)/shard_map/ppermute | solution.py:28
  55.8 5.2 %collective-permute-start.14 = (s32[32,128]{1,0:T(8,128)S(1)}, s32[32,128]{1,0:T(8,128)S(1)}, u32[]{:S(2)}, u32[]{:S(2)}) collective-permute-start(s32[32,128]{1,0:T(8,128)S(1)} %add.185), channel_id=1, source_target_pairs={{0,16},{1,17},{2,18},{3,19},{4,20},{5,21},{6,22},{7,23},{8,24},{9,... | collective-permute-start | bytes 49160 | tf_op jit(solution)/shard_map/ppermute | solution.py:28
  57.7 3.7 %collective-permute-start.13 = (s32[32,128]{1,0:T(8,128)S(1)}, s32[32,128]{1,0:T(8,128)S(1)}, u32[]{:S(2)}, u32[]{:S(2)}) collective-permute-start(s32[32,128]{1,0:T(8,128)S(1)} %add.185), channel_id=1, source_target_pairs={{0,8},{1,9},{2,10},{3,11},{4,12},{5,13},{6,14},{7,15},{8,0},{9,1},... | collective-permute-start | bytes 49160 | tf_op jit(solution)/shard_map/ppermute | solution.py:28
  61.5 6.0 %collective-permute-start.16 = (s32[128,128]{1,0:T(8,128)S(1)}, s32[128,128]{1,0:T(8,128)S(1)}, u32[]{:S(2)}, u32[]{:S(2)}) collective-permute-start(s32[128,128]{1,0:T(8,128)S(1)} %add_select_fusion.5), channel_id=1, source_target_pairs={{0,64},{1,65},{2,66},{3,67},{4,68},{5,69},{6,70},{7,71},{8,72},{9,... | collective-permute-start | bytes 196616 | tf_op jit(solution)/shard_map/ppermute | solution.py:28
  63.0 4.9 %collective-permute-start.19 = (bf16[512,512]{1,0:T(8,128)(2,1)}, bf16[512,512]{1,0:T(8,128)(2,1)S(1)}, u32[]{:S(2)}, u32[]{:S(2)}) collective-permute-start(bf16[512,512]{1,0:T(8,128)(2,1)} %get-tuple-element.106), channel_id=1, source_target_pairs={{0,1},{1,0},{2,3},{3,2},{4,5},{5,4},{6,7},{7,6},{8,9},{9,8},{10,11... | collective-permute-start | bytes 1572872 | tf_op jit(solution)/shard_map/ppermute | solution.py:28
  67.4 2.3 %collective-permute-start.18 = (bf16[512,512]{1,0:T(8,128)(2,1)}, bf16[512,512]{1,0:T(8,128)(2,1)}, u32[]{:S(2)}, u32[]{:S(2)}) collective-permute-start(bf16[512,512]{1,0:T(8,128)(2,1)} %get-tuple-element.107), channel_id=1, source_target_pairs={{0,1},{1,0},{2,3},{3,2},{4,5},{5,4},{6,7},{7,6},{8,9},{9,8},{10,11... | collective-permute-start | bytes 1572872 | tf_op jit(solution)/shard_map/ppermute | solution.py:28
  67.4 3.0 %collective-permute-start.17 = (bf16[512,512]{1,0:T(8,128)(2,1)}, bf16[512,512]{1,0:T(8,128)(2,1)}, u32[]{:S(2)}, u32[]{:S(2)}) collective-permute-start(bf16[512,512]{1,0:T(8,128)(2,1)} %get-tuple-element.108), channel_id=1, source_target_pairs={{0,1},{1,0},{2,3},{3,2},{4,5},{5,4},{6,7},{7,6},{8,9},{9,8},{10,11... | collective-permute-start | bytes 1572872 | tf_op jit(solution)/shard_map/ppermute | solution.py:28
  70.5 11.1 %collective-permute-start.21 = (s32[256,128]{1,0:T(8,128)S(1)}, s32[256,128]{1,0:T(8,128)S(1)}, u32[]{:S(2)}, u32[]{:S(2)}) collective-permute-start(s32[256,128]{1,0:T(8,128)S(1)} %add_select_fusion.4), channel_id=1, source_target_pairs={{0,128},{1,129},{2,130},{3,131},{4,132},{5,133},{6,134},{7,135},{8... | collective-permute-start | bytes 393224 | tf_op jit(solution)/shard_map/ppermute | solution.py:28
  70.6 23.0 %collective-permute-start.23 = (bf16[512,512]{1,0:T(8,128)(2,1)}, bf16[512,512]{1,0:T(8,128)(2,1)S(1)}, u32[]{:S(2)}, u32[]{:S(2)}) collective-permute-start(bf16[512,512]{1,0:T(8,128)(2,1)} %get-tuple-element.96), channel_id=1, source_target_pairs={{0,2},{1,3},{2,0},{3,1},{4,6},{5,7},{6,4},{7,5},{8,10},{9,11},{10,... | collective-permute-start | bytes 1572872 | tf_op jit(solution)/shard_map/ppermute | solution.py:28
  71.2 12.3 %copy-start = (f32[1536,512]{1,0:T(8,128)S(1)}, f32[1536,512]{1,0:T(8,128)}, u32[]{:S(2)}) copy-start(f32[1536,512]{1,0:T(8,128)} %get-tuple-element.97.own_ref) | copy-start | bytes 9437188
  85.3 8.3 %copy-start.1 = (f32[512,512]{1,0:T(8,128)S(1)}, f32[512,512]{1,0:T(8,128)}, u32[]{:S(2)}) copy-start(f32[512,512]{1,0:T(8,128)} %get-tuple-element.95.own_ref) | copy-start | bytes 3145732
  (5 other events, 14.6 us)

commit v4 on v3

--- a/solution.py
+++ b/solution.py
@@ -39,11 +39,19 @@
     return jnp.sum(jnp.where(match, values[None, :], jnp.float32(0.0)), axis=1)
 
 
+prime = 32749
+
+
 def dither_levels(seeds, fragment, lanes):
-    lane = jnp.arange(lanes, dtype=jnp.int32)
-    first = (seeds[:, None] + 7919 * lane[None, :] + 4099 * fragment) % 32749
-    second = (first * first + 3 * first + 17) % 32749
-    return second % 16
+    lane = (7919 * jnp.arange(lanes, dtype=jnp.int32)) % prime
+    row = (seeds + 4099 * fragment) % prime
+    first = row[:, None] + lane[None, :]
+    first = jnp.where(first >= prime, first - prime, first)
+    square = first * (first + 3) + 17
+    second = square - (square.astype(f32) * (1.0 / prime)).astype(jnp.int32) * prime
+    second = jnp.where(second < 0, second + prime, second)
+    second = jnp.where(second >= prime, second - prime, second)
+    return second & 15
 
 
 def norm_kernel(me_ref, x_ref, gain_ref, near_ref, f0_ref, f1_ref, f2_ref, f3_ref, inv_ref):
@@ -91,7 +99,7 @@
         out_shape=[pltpu.HBM((2, rows, slab), bf16)]
         + [pltpu.HBM((rows, slab // 2), bf16)] * 4
         + [jax.ShapeDtypeStruct((rows, 128), f32)],
-        compiler_params=params(),
+        compiler_params=params(24),
         cost_estimate=small,
         name="norm",
     )(me, hidden, gain)
@@ -128,8 +136,8 @@
             pl.BlockSpec((tokens, width), fixed),
         ],
         out_specs=[pl.BlockSpec((rows, width), fixed) for rows in counts],
-        out_shape=[pltpu.HBM((rows, width), dtype) for rows in counts],
-        compiler_params=params(),
+        out_shape=[jax.ShapeDtypeStruct((rows, width), dtype) for rows in counts],
+        compiler_params=params(24),
         cost_estimate=small,
         name=name,
     )(mine, theirs[2 * place], theirs[2 * place + 1], cot, cot_theirs)
@@ -245,7 +253,7 @@
             pltpu.SemaphoreType.DMA((7 + pieces,)),
             pltpu.SemaphoreType.DMA((8,)),
         ],
-        compiler_params=params(),
+        compiler_params=params(40),
         cost_estimate=small,
         name="keys_and_input_grad",
     )(me, *whole, *parts, hidden, gain, cot, inv)
@@ -345,26 +353,26 @@
     level = level_table(scale_exponents)[:, None]
     total = packed_codes(global_base, replica_params, level, dither_seeds, fragment_index)
     total, hidden = lax.optimization_barrier((total, hidden_in))
-    total, (near, far, inv) = halve(total, 4, lambda: norm_slabs(me, hidden, gain))
-    total, came = halve(total, 2, lambda: [send(part, core_bit) for part in far])
-    total, out_rows = scatter_y(
-        total, lambda: grad_rows(near, came, key_cot, cot_sibling, 1, bf16, "grad_out")
-    )
-    in_rows = [send(rows, x_lo_bit) for rows in out_rows]
-    total, own_rows = exchange(
+    total, (near, far, inv) = halve(total, 2, lambda: norm_slabs(me, hidden, gain))
+    total, came = scatter_y(total, lambda: [send(part, core_bit) for part in far])
+    total, out_rows = exchange(
         total,
         x_hi_bit | z_bit,
-        lambda: grad_rows(near, came, key_cot, cot_sibling, 0, f32, "grad_own"),
-    )
+        lambda: grad_rows(near, came, key_cot, cot_sibling, 1, bf16, "grad_out"),
+    )
+    in_rows = [send(rows, x_lo_bit) for rows in out_rows]
     total, _ = exchange(total, z_bit, nothing)
+    total, _ = exchange(total, z_bit * 4, nothing)
     total, partner = lax.optimization_barrier((total, partner))
     quarter = partner.shape[0] // pieces
     diagonal = [send(partner[k * quarter : (k + 1) * quarter], core_bit) for k in range(pieces)]
-    total, _ = gather_y(total, nothing)
-    total, diagonal = gather_z(total, 2, lambda: diagonal)
+    total, (diagonal, own_rows) = gather_y(
+        total,
+        lambda: (diagonal, grad_rows(near, came, key_cot, cot_sibling, 0, f32, "grad_own")),
+    )
     total, (keys, input_grad) = gather_z(
         total,
-        4,
+        2,
         lambda: token_outputs(
             me, (own, sibling, partner), diagonal, hidden, gain, key_cot, inv
         ),

time: 94.9 us -> 95.3 us (level)
  local copies, waits for them, and re-layouts: 3.2 us -> 10.1 us
  Pallas kernels: 27.6 us -> 21.7 us
  other arithmetic: 6.56 us -> 5.39 us
  waiting for transfers between devices: 34.2 us -> 35.2 us
    unnamed x24, local copies, waits for them, and re-layouts: 0.29 us -> 8.87 us
    pallas_call x2, Pallas kernels: 8.74 us -> 5.85 us  [grad_rows(): pl.pallas_call(grad_kernel, grid=(1,), in_specs=[pl.BlockSpec((1, tokens,...]
    pallas_call x1, Pallas kernels: 10.3 us -> 7.8 us  [token_outputs(): pl.pallas_call(token_kernel, in_specs=[pl.BlockSpec(memory_space=pltpu.SM...]
    pallas_call x1, Pallas kernels: 5.87 us -> 3.61 us  [norm_slabs(): pl.pallas_call(norm_kernel, grid_spec=pltpu.PrefetchScalarGridSpec(num_sc...]
    pallas_call x2, Pallas kernels: 2.67 us -> 4.43 us  [add_rows(): pl.pallas_call(add_kernel, grid=(rows // block,), in_specs=[part, part] +...]
    slice x1, local copies, waits for them, and re-layouts: 2.86 us -> 1.17 us  [per_device(): partner[k * quarter:(k + 1) * quarter]]
    add x1, other arithmetic: 3.39 us -> 2.19 us  [packed_codes(): shifted = code + 8]
    ppermute x25 -> x24, waiting for transfers between devices: 34.2 us -> 35.2 us  [send(): return lax.ppermute(value, axes, flip(bit))]
  transfers between devices with their start and end apart: 25 -> 24, of which waited for: 13 -> 13; matrix products, arithmetic and copies ran while one was open for 10% -> 7% of each run, Pallas kernels for 28% -> 22%
where the time goes in v4:
time: 95.3 us; the launch traced here: 94.8 us
  waiting for transfers between devices  35.2 us (37%)
  Pallas kernels  21.7 us (23%)
  starting transfers between devices  20.9 us (22%)
  local copies, waits for them, and re-layouts  10.1 us (11%)
  other arithmetic  5.39 us (6%)
  between operations  1.5 us (2%)
    ppermute x24, waiting for transfers between devices, send(): return lax.ppermute(value, axes, flip(bit))  35.2 us
    ppermute x24, starting transfers between devices, send(): return lax.ppermute(value, axes, flip(bit))  20.9 us
    unnamed x24, local copies, waits for them, and re-layouts  8.87 us
    pallas_call x1, Pallas kernels, token_outputs(): pl.pallas_call(token_kernel, in_specs=[pl.BlockSpec(memory_space=pltpu.SM...  7.8 us
    pallas_call x2, Pallas kernels, grad_rows(): pl.pallas_call(grad_kernel, grid=(1,), in_specs=[pl.BlockSpec((1, tokens,...  5.85 us
    pallas_call x2, Pallas kernels, add_rows(): pl.pallas_call(add_kernel, grid=(rows // block,), in_specs=[part, part] +...  4.43 us
    pallas_call x1, Pallas kernels, norm_slabs(): pl.pallas_call(norm_kernel, grid_spec=pltpu.PrefetchScalarGridSpec(num_sc...  3.61 us
    add x1, other arithmetic, packed_codes(): shifted = code + 8  2.19 us
  transfers between devices with their start and end apart: 24, of which 13 were waited for; matrix products, arithmetic and copies ran while one was open for 7% of the time, Pallas kernels for 22%

profile of v4, /device:TPU:130, one launch (start us, length us, event | category | flops | bytes accessed | tf_op | source)
XLA Modules:
  0.0 94.8 jit_solution(12631166295109891552)
XLA Ops:
  3.5 2.2 %fusion.9 = s32[1536,128]{1,0:T(8,128)S(1)} fusion(f32[1536,128]{1,0:T(8,128)} %param.15, bf16[1,1536,128]{2,1,0:T(8,128)(2,1)} %param.16, s32[128]{0:T(128)S(1)} %and_select_fusion, s32[1536]{0:T(1024)S(1)} %add_select_fusion.4, f32[1536]{0:T(1024)S(1)} %select_reduce_fusion), kind=kLoop, calls=%fused_computation.13 | loop fusion | flops 5898240 | bytes 1978880 | tf_op jit(solution)/shard_map/add | solution.py:268
  5.8 1.6 %collective-permute-start = (s32[256,128]{1,0:T(8,128)S(1)}, s32[256,128]{1,0:T(8,128)S(1)}, u32[]{:S(2)}, u32[]{:S(2)}) collective-permute-start(s32[256,128]{1,0:T(8,128)S(1)} %constant_dynamic-slice_fusion.3), channel_id=1, source_target_pairs={{0,64},{1,65},{2,66},{3,67},{4,68},{5,69},{6,70},{7,71},{8,72},{9,... | collective-permute-start | bytes 393224 | tf_op jit(solution)/shard_map/ppermute | solution.py:28
  7.3 2.2 %copy-done = bf16[256,8192]{1,0:T(8,128)(2,1)S(1)} copy-done((bf16[256,8192]{1,0:T(8,128)(2,1)S(1)}, bf16[256,8192]{1,0:T(8,128)(2,1)}, u32[]{:S(2)}) %copy-start) | copy-done | bytes 4194328
  9.5 3.6 %norm.1 = (bf16[2,256,2048]{2,1,0:T(8,128)(2,1)}, bf16[256,1024]{1,0:T(8,128)(2,1)}, bf16[256,1024]{1,0:T(8,128)(2,1)}, bf16[256,1024]{1,0:T(8,128)(2,1)}, bf16[...) custom-call(s32[1]{0:T(128)} %bitcast.2.me_ref, bf16[256,8192]{1,0:T(8,128)(2,1)S(1)} %copy-done, f32[1,8192]{1,0:T(1,128)S(1)} %bitcast.10), custom_call_target="tpu_custom_call" | custom-call | flops 1024 | bytes 1024 | tf_op jit(solution)/shard_map/norm/pallas_call | solution.py:86
  13.1 1.4 %collective-permute-done = s32[256,128]{1,0:T(8,128)S(1)} collective-permute-done((s32[256,128]{1,0:T(8,128)S(1)}, s32[256,128]{1,0:T(8,128)S(1)}, u32[]{:S(2)}, u32[]{:S(2)}) %collective-permute-start) | collective-permute-done | bytes 131104 | tf_op jit(solution)/shard_map/ppermute | solution.py:28
  14.6 3.1 %collective-permute-start.3 = (s32[64,128]{1,0:T(8,128)S(1)}, s32[64,128]{1,0:T(8,128)S(1)}, u32[]{:S(2)}, u32[]{:S(2)}) collective-permute-start(s32[64,128]{1,0:T(8,128)S(1)} %get-tuple-element.108), channel_id=1, source_target_pairs={{0,24},{1,25},{2,26},{3,27},{4,28},{5,29},{6,30},{7,31},{8,16},{9,... | collective-permute-start | bytes 98312 | tf_op jit(solution)/shard_map/ppermute | solution.py:28
  19.8 3.3 %collective-permute-done.2 = s32[64,128]{1,0:T(8,128)S(1)} collective-permute-done((s32[64,128]{1,0:T(8,128)S(1)}, s32[64,128]{1,0:T(8,128)S(1)}, u32[]{:S(2)}, u32[]{:S(2)}) %collective-permute-start.2) | collective-permute-done | bytes 32800 | tf_op jit(solution)/shard_map/ppermute | solution.py:28
  24.1 1.2 %collective-permute-done.6.low_ref = bf16[256,1024]{1,0:T(8,128)(2,1)} collective-permute-done((bf16[256,1024]{1,0:T(8,128)(2,1)}, bf16[256,1024]{1,0:T(8,128)(2,1)}, u32[]{:S(2)}, u32[]{:S(2)}) %collective-permute-start.6) | collective-permute-done | bytes 524320 | tf_op jit(solution)/shard_map/ppermute | solution.py:28
  25.4 1.1 %collective-permute-done.7.high_ref = bf16[256,1024]{1,0:T(8,128)(2,1)} collective-permute-done((bf16[256,1024]{1,0:T(8,128)(2,1)}, bf16[256,1024]{1,0:T(8,128)(2,1)}, u32[]{:S(2)}, u32[]{:S(2)}) %collective-permute-start.7) | collective-permute-done | bytes 524320 | tf_op jit(solution)/shard_map/ppermute | solution.py:28
  26.5 1.6 %collective-permute-start.8 = (s32[64,128]{1,0:T(8,128)S(1)}, s32[64,128]{1,0:T(8,128)S(1)}, u32[]{:S(2)}, u32[]{:S(2)}) collective-permute-start(s32[64,128]{1,0:T(8,128)S(1)} %add_add_fusion.1), channel_id=1, source_target_pairs={{0,36},{1,37},{2,38},{3,39},{4,32},{5,33},{6,34},{7,35},{8,44},{9,... | collective-permute-start | bytes 98312 | tf_op jit(solution)/shard_map/ppermute | solution.py:28
  28.1 1.6 %copy-done.2 = bf16[2,256,2048]{2,1,0:T(8,128)(2,1)S(1)} copy-done((bf16[2,256,2048]{2,1,0:T(8,128)(2,1)S(1)}, bf16[2,256,2048]{2,1,0:T(8,128)(2,1)}, u32[]{:S(2)}) %copy-start.2) | copy-done | bytes 2097176
  29.7 3.4 %grad_out.1 = (bf16[1536,512]{1,0:T(8,128)(2,1)}, bf16[512,512]{1,0:T(8,128)(2,1)S(1)}) custom-call(bf16[2,256,2048]{2,1,0:T(8,128)(2,1)S(1)} %copy-done.2, bf16[256,1024]{1,0:T(8,128)(2,1)} %collective-permute-done.6.low_ref, bf16[256,1024]{1,0:T(8,128)(2,1)} %collective-permute-done.7.high_ref, bf16[256,512]{1,0:T(8,128)(2,1)S(1)} %copy-done.4, ...), custom_call_target="tpu_custom_call" | custom-call | flops 1024 | bytes 1024 | tf_op jit(solution)/shard_map/grad_out/pallas_call | solution.py:128
  33.0 2.5 %collective-permute-start.10 = (s32[64,128]{1,0:T(8,128)S(1)}, s32[64,128]{1,0:T(8,128)S(1)}, u32[]{:S(2)}, u32[]{:S(2)}) collective-permute-start(s32[64,128]{1,0:T(8,128)S(1)} %add.185), channel_id=1, source_target_pairs={{0,32},{1,33},{2,34},{3,35},{4,36},{5,37},{6,38},{7,39},{8,40},{9,... | collective-permute-start | bytes 98312 | tf_op jit(solution)/shard_map/ppermute | solution.py:28
  35.5 1.9 %collective-permute-done.10 = s32[64,128]{1,0:T(8,128)S(1)} collective-permute-done((s32[64,128]{1,0:T(8,128)S(1)}, s32[64,128]{1,0:T(8,128)S(1)}, u32[]{:S(2)}, u32[]{:S(2)}) %collective-permute-start.10) | collective-permute-done | bytes 32800 | tf_op jit(solution)/shard_map/ppermute | solution.py:28
  37.4 1.1 %collective-permute-start.11 = (s32[64,128]{1,0:T(8,128)S(1)}, s32[64,128]{1,0:T(8,128)S(1)}, u32[]{:S(2)}, u32[]{:S(2)}) collective-permute-start(s32[64,128]{1,0:T(8,128)S(1)} %add.186), channel_id=1, source_target_pairs={{0,128},{1,129},{2,130},{3,131},{4,132},{5,133},{6,134},{7,135},{8... | collective-permute-start | bytes 98312 | tf_op jit(solution)/shard_map/ppermute | solution.py:28
  38.5 1.8 %collective-permute-start.23 = (bf16[1536,512]{1,0:T(8,128)(2,1)}, bf16[1536,512]{1,0:T(8,128)(2,1)}, u32[]{:S(2)}, u32[]{:S(2)}) collective-permute-start(bf16[1536,512]{1,0:T(8,128)(2,1)} %get-tuple-element.95), channel_id=1, source_target_pairs={{0,2},{1,3},{2,0},{3,1},{4,6},{5,7},{6,4},{7,5},{8,10},{9,11},{10,... | collective-permute-start | bytes 4718600 | tf_op jit(solution)/shard_map/ppermute | solution.py:28
  40.3 5.0 %collective-permute-done.11 = s32[64,128]{1,0:T(8,128)S(1)} collective-permute-done((s32[64,128]{1,0:T(8,128)S(1)}, s32[64,128]{1,0:T(8,128)S(1)}, u32[]{:S(2)}, u32[]{:S(2)}) %collective-permute-start.11) | collective-permute-done | bytes 32800 | tf_op jit(solution)/shard_map/ppermute | solution.py:28
  45.3 4.9 %collective-permute-done.12.refs_2_ = bf16[2048,512]{1,0:T(8,128)(2,1)S(1)} collective-permute-done((bf16[2048,512]{1,0:T(8,128)(2,1)}, bf16[2048,512]{1,0:T(8,128)(2,1)S(1)}, u32[]{:S(2)}, u32[]{:S(2)}) %collective-permute-start.12) | collective-permute-done | bytes 2097184 | tf_op jit(solution)/shard_map/ppermute | solution.py:28
  50.2 1.2 %fusion.15 = (bf16[512,512]{1,0:T(8,128)(2,1)S(1)}, bf16[512,512]{1,0:T(8,128)(2,1)}, bf16[512,512]{1,0:T(8,128)(2,1)}, bf16[512,512]{1,0:T(8,128)(2,1)}) fusion(bf16[2048,512]{1,0:T(8,128)(2,1)S(1)} %collective-permute-done.12.refs_2_), kind=kLoop, calls=%fused_computation.44 | loop fusion | bytes 4194304 | tf_op jit(solution)/shard_map/slice | solution.py:368
  51.3 3.0 %collective-permute-start.15 = (s32[64,128]{1,0:T(8,128)S(1)}, s32[64,128]{1,0:T(8,128)S(1)}, u32[]{:S(2)}, u32[]{:S(2)}) collective-permute-start(s32[64,128]{1,0:T(8,128)S(1)} %add.187), channel_id=1, source_target_pairs={{0,24},{1,25},{2,26},{3,27},{4,28},{5,29},{6,30},{7,31},{8,16},{9,... | collective-permute-start | bytes 98312 | tf_op jit(solution)/shard_map/ppermute | solution.py:28
  55.0 1.5 %collective-permute-done.15 = s32[64,128]{1,0:T(8,128)S(1)} collective-permute-done((s32[64,128]{1,0:T(8,128)S(1)}, s32[64,128]{1,0:T(8,128)S(1)}, u32[]{:S(2)}, u32[]{:S(2)}) %collective-permute-start.15) | collective-permute-done | bytes 32800 | tf_op jit(solution)/shard_map/ppermute | solution.py:28
  56.8 2.9 %collective-permute-done.14 = s32[64,128]{1,0:T(8,128)S(1)} collective-permute-done((s32[64,128]{1,0:T(8,128)S(1)}, s32[64,128]{1,0:T(8,128)S(1)}, u32[]{:S(2)}, u32[]{:S(2)}) %collective-permute-start.14) | collective-permute-done | bytes 32800 | tf_op jit(solution)/shard_map/ppermute | solution.py:28
  61.7 1.6 %copy-done.3 = bf16[2,256,2048]{2,1,0:T(8,128)(2,1)S(1)} copy-done((bf16[2,256,2048]{2,1,0:T(8,128)(2,1)S(1)}, bf16[2,256,2048]{2,1,0:T(8,128)(2,1)}, u32[]{:S(2)}) %copy-start.3) | copy-done | bytes 2097176
  63.3 2.5 %grad_own.1 = (f32[1536,512]{1,0:T(8,128)S(1)}, f32[512,512]{1,0:T(8,128)S(1)}) custom-call(bf16[2,256,2048]{2,1,0:T(8,128)(2,1)S(1)} %copy-done.3, bf16[256,1024]{1,0:T(8,128)(2,1)S(1)} %collective-permute-done.4.low_ref, bf16[256,1024]{1,0:T(8,128)(2,1)} %collective-permute-done.5.high_ref, bf16[256,512]{1,0:T(8,128)(2,1)S(1)} %copy-done.4, ...), custom_call_target="tpu_custom_call" | custom-call | flops 1024 | bytes 1024 | tf_op jit(solution)/shard_map/grad_own/pallas_call | solution.py:128
  65.9 1.6 %collective-permute-start.20 = (s32[256,128]{1,0:T(8,128)S(1)}, s32[256,128]{1,0:T(8,128)S(1)}, u32[]{:S(2)}, u32[]{:S(2)}) collective-permute-start(s32[256,128]{1,0:T(8,128)S(1)} %add_select_fusion.1), channel_id=1, source_target_pairs={{0,64},{1,65},{2,66},{3,67},{4,68},{5,69},{6,70},{7,71},{8,72},{9,... | collective-permute-start | bytes 393224 | tf_op jit(solution)/shard_map/ppermute | solution.py:28
  68.0 1.6 %copy-done.5 = bf16[1,2048,512]{2,1,0:T(8,128)(2,1)S(1)} copy-done((bf16[1,2048,512]{2,1,0:T(8,128)(2,1)S(1)}, bf16[1,2048,512]{2,1,0:T(8,128)(2,1)}, u32[]{:S(2)}) %copy-start.5) | copy-done | bytes 2097176
  69.6 1.0 %copy-done.7 = bf16[512,512]{1,0:T(8,128)(2,1)S(1)} copy-done((bf16[512,512]{1,0:T(8,128)(2,1)S(1)}, bf16[512,512]{1,0:T(8,128)(2,1)}, u32[]{:S(2)}) %copy-start.7) | copy-done | bytes 524312
  70.6 7.8 %keys_and_input_grad.1 = (bf16[256,512]{1,0:T(8,128)(2,1)}, bf16[256,8192]{1,0:T(8,128)(2,1)}) custom-call(s32[1]{0:T(128)} %bitcast.2.me_ref, bf16[2048,512]{1,0:T(8,128)(2,1)S(1)} %bitcast.9, bf16[2048,512]{1,0:T(8,128)(2,1)} %collective-permute-done.21.refs_1_, bf16[2048,512]{1,0:T(8,128)(2,1)S(1)} %collective-permute-done.12.refs_2_, ...), custom_call_target="tpu_custom_call" | custom-call | flops 1024 | bytes 1024 | tf_op jit(solution)/shard_map/keys_and_input_grad/pallas_call | solution.py:241
  78.5 5.5 %collective-permute-done.23.came_ref = bf16[1536,512]{1,0:T(8,128)(2,1)} collective-permute-done((bf16[1536,512]{1,0:T(8,128)(2,1)}, bf16[1536,512]{1,0:T(8,128)(2,1)}, u32[]{:S(2)}, u32[]{:S(2)}) %collective-permute-start.23) | collective-permute-done | bytes 1572896 | tf_op jit(solution)/shard_map/ppermute | solution.py:28
  84.0 3.5 %add.312.refs_0_ = bf16[1,2048,512]{2,1,0:T(8,128)(2,1)} custom-call(f32[1536,512]{1,0:T(8,128)S(1)} %get-tuple-element.93.own_ref, bf16[1536,512]{1,0:T(8,128)(2,1)} %collective-permute-done.23.came_ref), custom_call_target="tpu_custom_call" | custom-call | flops 1024 | bytes 1024 | tf_op jit(solution)/shard_map/add/pallas_call | solution.py:155
  87.6 1.5 %multiply_subtract_fusion = (f32[1536,128]{1,0:T(8,128)}, f32[1536,128]{1,0:T(8,128)}) fusion(f32[1536,128]{1,0:T(8,128)S(1)} %copy-done.10, s32[512,128]{1,0:T(8,128)S(1)} %get-tuple-element.107, s32[512,128]{1,0:T(8,128)S(1)} %get-tuple-element.106, s32[512,128]{1,0:T(8,128)S(1)} %get-tuple-element.105, f32[1536]{0:T(1024)S(1)} %divide_multiply_fusion, ...), kind=kLoop, calls=%fused_computation.19 | loop fusion | flops 2162688 | bytes 3938304 | tf_op jit(solution)/shard_map/sub | solution.py:329
  89.1 4.9 %collective-permute-done.22.came_ref = bf16[512,512]{1,0:T(8,128)(2,1)S(1)} collective-permute-done((bf16[512,512]{1,0:T(8,128)(2,1)}, bf16[512,512]{1,0:T(8,128)(2,1)S(1)}, u32[]{:S(2)}, u32[]{:S(2)}) %collective-permute-start.22) | collective-permute-done | bytes 524320 | tf_op jit(solution)/shard_map/ppermute | solution.py:28
  (66 shorter events, 10.0 us)
Async XLA Ops:
  0.6 6.7 %copy-start.8 = (f32[8192]{0:T(1024)S(1)}, f32[8192]{0:T(1024)}, u32[]{:S(2)}) copy-start(f32[8192]{0:T(1024)} %param.12) | copy-start | bytes 98308
  0.6 49.5 %collective-permute-start.12 = (bf16[2048,512]{1,0:T(8,128)(2,1)}, bf16[2048,512]{1,0:T(8,128)(2,1)S(1)}, u32[]{:S(2)}, u32[]{:S(2)}) collective-permute-start(bf16[2048,512]{1,0:T(8,128)(2,1)} %bitcast.7), channel_id=1, source_target_pairs={{0,2},{1,3},{2,0},{3,1},{4,6},{5,7},{6,4},{7,5},{8,10},{9,11},{10,... | collective-permute-start | bytes 6291464 | tf_op jit(solution)/shard_map/ppermute | solution.py:28
  5.8 8.8 %collective-permute-start = (s32[256,128]{1,0:T(8,128)S(1)}, s32[256,128]{1,0:T(8,128)S(1)}, u32[]{:S(2)}, u32[]{:S(2)}) collective-permute-start(s32[256,128]{1,0:T(8,128)S(1)} %constant_dynamic-slice_fusion.3), channel_id=1, source_target_pairs={{0,64},{1,65},{2,66},{3,67},{4,68},{5,69},{6,70},{7,71},{8,72},{9,... | collective-permute-start | bytes 393224 | tf_op jit(solution)/shard_map/ppermute | solution.py:28
  7.3 2.2 %copy-start = (bf16[256,8192]{1,0:T(8,128)(2,1)S(1)}, bf16[256,8192]{1,0:T(8,128)(2,1)}, u32[]{:S(2)}) copy-start(bf16[256,8192]{1,0:T(8,128)(2,1)} %refs_7_) | copy-start | bytes 12582916
  9.5 14.1 %copy-start.4 = (bf16[256,512]{1,0:T(8,128)(2,1)S(1)}, bf16[256,512]{1,0:T(8,128)(2,1)}, u32[]{:S(2)}) copy-start(bf16[256,512]{1,0:T(8,128)(2,1)} %refs_9_.1) | copy-start | bytes 786436
  14.6 5.2 %collective-permute-start.3 = (s32[64,128]{1,0:T(8,128)S(1)}, s32[64,128]{1,0:T(8,128)S(1)}, u32[]{:S(2)}, u32[]{:S(2)}) collective-permute-start(s32[64,128]{1,0:T(8,128)S(1)} %get-tuple-element.108), channel_id=1, source_target_pairs={{0,24},{1,25},{2,26},{3,27},{4,28},{5,29},{6,30},{7,31},{8,16},{9,... | collective-permute-start | bytes 98312 | tf_op jit(solution)/shard_map/ppermute | solution.py:28
  17.7 5.4 %collective-permute-start.2 = (s32[64,128]{1,0:T(8,128)S(1)}, s32[64,128]{1,0:T(8,128)S(1)}, u32[]{:S(2)}, u32[]{:S(2)}) collective-permute-start(s32[64,128]{1,0:T(8,128)S(1)} %get-tuple-element.109), channel_id=1, source_target_pairs={{0,16},{1,17},{2,18},{3,19},{4,20},{5,21},{6,22},{7,23},{8,24},{9,... | collective-permute-start | bytes 98312 | tf_op jit(solution)/shard_map/ppermute | solution.py:28
  18.3 4.8 %collective-permute-start.1 = (s32[64,128]{1,0:T(8,128)S(1)}, s32[64,128]{1,0:T(8,128)S(1)}, u32[]{:S(2)}, u32[]{:S(2)}) collective-permute-start(s32[64,128]{1,0:T(8,128)S(1)} %get-tuple-element.110), channel_id=1, source_target_pairs={{0,8},{1,9},{2,10},{3,11},{4,12},{5,13},{6,14},{7,15},{8,0},{9,1},... | collective-permute-start | bytes 98312 | tf_op jit(solution)/shard_map/ppermute | solution.py:28
  18.8 4.9 %collective-permute-start.4 = (bf16[256,1024]{1,0:T(8,128)(2,1)}, bf16[256,1024]{1,0:T(8,128)(2,1)S(1)}, u32[]{:S(2)}, u32[]{:S(2)}) collective-permute-start(bf16[256,1024]{1,0:T(8,128)(2,1)} %get-tuple-element.61), channel_id=1, source_target_pairs={{0,1},{1,0},{2,3},{3,2},{4,5},{5,4},{6,7},{7,6},{8,9},{9,8},{10,11... | collective-permute-start | bytes 1572872 | tf_op jit(solution)/shard_map/ppermute | solution.py:28
  19.8 3.9 %collective-permute-start.5 = (bf16[256,1024]{1,0:T(8,128)(2,1)}, bf16[256,1024]{1,0:T(8,128)(2,1)}, u32[]{:S(2)}, u32[]{:S(2)}) collective-permute-start(bf16[256,1024]{1,0:T(8,128)(2,1)} %get-tuple-element.62), channel_id=1, source_target_pairs={{0,1},{1,0},{2,3},{3,2},{4,5},{5,4},{6,7},{7,6},{8,9},{9,8},{10,11... | collective-permute-start | bytes 1572872 | tf_op jit(solution)/shard_map/ppermute | solution.py:28
  23.1 2.3 %collective-permute-start.6 = (bf16[256,1024]{1,0:T(8,128)(2,1)}, bf16[256,1024]{1,0:T(8,128)(2,1)}, u32[]{:S(2)}, u32[]{:S(2)}) collective-permute-start(bf16[256,1024]{1,0:T(8,128)(2,1)} %get-tuple-element.63), channel_id=1, source_target_pairs={{0,1},{1,0},{2,3},{3,2},{4,5},{5,4},{6,7},{7,6},{8,9},{9,8},{10,11... | collective-permute-start | bytes 1572872 | tf_op jit(solution)/shard_map/ppermute | solution.py:28
  23.1 3.4 %collective-permute-start.7 = (bf16[256,1024]{1,0:T(8,128)(2,1)}, bf16[256,1024]{1,0:T(8,128)(2,1)}, u32[]{:S(2)}, u32[]{:S(2)}) collective-permute-start(bf16[256,1024]{1,0:T(8,128)(2,1)} %get-tuple-element.64), channel_id=1, source_target_pairs={{0,1},{1,0},{2,3},{3,2},{4,5},{5,4},{6,7},{7,6},{8,9},{9,8},{10,11... | collective-permute-start | bytes 1572872 | tf_op jit(solution)/shard_map/ppermute | solution.py:28
  23.6 4.5 %collective-permute-start.9 = (bf16[256,512]{1,0:T(8,128)(2,1)S(1)}, bf16[256,512]{1,0:T(8,128)(2,1)S(1)}, u32[]{:S(2)}, u32[]{:S(2)}) collective-permute-start(bf16[256,512]{1,0:T(8,128)(2,1)S(1)} %copy-done.4), channel_id=1, source_target_pairs={{0,1},{1,0},{2,3},{3,2},{4,5},{5,4},{6,7},{7,6},{8,9},{9,8},{10,11... | collective-permute-start | bytes 786440 | tf_op jit(solution)/shard_map/ppermute | solution.py:28
  23.7 44.3 %collective-permute-start.21 = (bf16[2048,512]{1,0:T(8,128)(2,1)}, bf16[2048,512]{1,0:T(8,128)(2,1)}, u32[]{:S(2)}, u32[]{:S(2)}) collective-permute-start(bf16[2048,512]{1,0:T(8,128)(2,1)} %bitcast.8), channel_id=1, source_target_pairs={{0,1},{1,0},{2,3},{3,2},{4,5},{5,4},{6,7},{7,6},{8,9},{9,8},{10,11... | collective-permute-start | bytes 6291464 | tf_op jit(solution)/shard_map/ppermute | solution.py:28
  26.5 6.5 %collective-permute-start.8 = (s32[64,128]{1,0:T(8,128)S(1)}, s32[64,128]{1,0:T(8,128)S(1)}, u32[]{:S(2)}, u32[]{:S(2)}) collective-permute-start(s32[64,128]{1,0:T(8,128)S(1)} %add_add_fusion.1), channel_id=1, source_target_pairs={{0,36},{1,37},{2,38},{3,39},{4,32},{5,33},{6,34},{7,35},{8,44},{9,... | collective-permute-start | bytes 98312 | tf_op jit(solution)/shard_map/ppermute | solution.py:28
  33.0 18.3 %copy-start.9 = (bf16[512,512]{1,0:T(8,128)(2,1)}, bf16[512,512]{1,0:T(8,128)(2,1)S(1)}, u32[]{:S(2)}) copy-start(bf16[512,512]{1,0:T(8,128)(2,1)S(1)} %get-tuple-element.92) | copy-start | bytes 1572868
  33.0 4.4 %collective-permute-start.10 = (s32[64,128]{1,0:T(8,128)S(1)}, s32[64,128]{1,0:T(8,128)S(1)}, u32[]{:S(2)}, u32[]{:S(2)}) collective-permute-start(s32[64,128]{1,0:T(8,128)S(1)} %add.185), channel_id=1, source_target_pairs={{0,32},{1,33},{2,34},{3,35},{4,36},{5,37},{6,38},{7,39},{8,40},{9,... | collective-permute-start | bytes 98312 | tf_op jit(solution)/shard_map/ppermute | solution.py:28
  37.4 7.8 %collective-permute-start.11 = (s32[64,128]{1,0:T(8,128)S(1)}, s32[64,128]{1,0:T(8,128)S(1)}, u32[]{:S(2)}, u32[]{:S(2)}) collective-permute-start(s32[64,128]{1,0:T(8,128)S(1)} %add.186), channel_id=1, source_target_pairs={{0,128},{1,129},{2,130},{3,131},{4,132},{5,133},{6,134},{7,135},{8... | collective-permute-start | bytes 98312 | tf_op jit(solution)/shard_map/ppermute | solution.py:28
  38.5 45.5 %collective-permute-start.23 = (bf16[1536,512]{1,0:T(8,128)(2,1)}, bf16[1536,512]{1,0:T(8,128)(2,1)}, u32[]{:S(2)}, u32[]{:S(2)}) collective-permute-start(bf16[1536,512]{1,0:T(8,128)(2,1)} %get-tuple-element.95), channel_id=1, source_target_pairs={{0,2},{1,3},{2,0},{3,1},{4,6},{5,7},{6,4},{7,5},{8,10},{9,11},{10,... | collective-permute-start | bytes 4718600 | tf_op jit(solution)/shard_map/ppermute | solution.py:28
  51.3 9.1 %collective-permute-start.19 = (bf16[512,512]{1,0:T(8,128)(2,1)S(1)}, bf16[512,512]{1,0:T(8,128)(2,1)S(1)}, u32[]{:S(2)}, u32[]{:S(2)}) collective-permute-start(bf16[512,512]{1,0:T(8,128)(2,1)S(1)} %get-tuple-element.101), channel_id=1, source_target_pairs={{0,1},{1,0},{2,3},{3,2},{4,5},{5,4},{6,7},{7,6},{8,9},{9,8},{10,11... | collective-permute-start | bytes 1572872 | tf_op jit(solution)/shard_map/ppermute | solution.py:28
  51.3 5.1 %collective-permute-start.15 = (s32[64,128]{1,0:T(8,128)S(1)}, s32[64,128]{1,0:T(8,128)S(1)}, u32[]{:S(2)}, u32[]{:S(2)}) collective-permute-start(s32[64,128]{1,0:T(8,128)S(1)} %add.187), channel_id=1, source_target_pairs={{0,24},{1,25},{2,26},{3,27},{4,28},{5,29},{6,30},{7,31},{8,16},{9,... | collective-permute-start | bytes 98312 | tf_op jit(solution)/shard_map/ppermute | solution.py:28
  54.4 5.4 %collective-permute-start.14 = (s32[64,128]{1,0:T(8,128)S(1)}, s32[64,128]{1,0:T(8,128)S(1)}, u32[]{:S(2)}, u32[]{:S(2)}) collective-permute-start(s32[64,128]{1,0:T(8,128)S(1)} %add.187), channel_id=1, source_target_pairs={{0,16},{1,17},{2,18},{3,19},{4,20},{5,21},{6,22},{7,23},{8,24},{9,... | collective-permute-start | bytes 98312 | tf_op jit(solution)/shard_map/ppermute | solution.py:28
  56.5 3.9 %collective-permute-start.13 = (s32[64,128]{1,0:T(8,128)S(1)}, s32[64,128]{1,0:T(8,128)S(1)}, u32[]{:S(2)}, u32[]{:S(2)}) collective-permute-start(s32[64,128]{1,0:T(8,128)S(1)} %add.187), channel_id=1, source_target_pairs={{0,8},{1,9},{2,10},{3,11},{4,12},{5,13},{6,14},{7,15},{8,0},{9,1},... | collective-permute-start | bytes 98312 | tf_op jit(solution)/shard_map/ppermute | solution.py:28
  59.8 6.0 %collective-permute-start.18 = (bf16[512,512]{1,0:T(8,128)(2,1)}, bf16[512,512]{1,0:T(8,128)(2,1)}, u32[]{:S(2)}, u32[]{:S(2)}) collective-permute-start(bf16[512,512]{1,0:T(8,128)(2,1)} %get-tuple-element.102), channel_id=1, source_target_pairs={{0,1},{1,0},{2,3},{3,2},{4,5},{5,4},{6,7},{7,6},{8,9},{9,8},{10,11... | collective-permute-start | bytes 1572872 | tf_op jit(solution)/shard_map/ppermute | solution.py:28
  60.4 5.4 %collective-permute-start.17 = (bf16[512,512]{1,0:T(8,128)(2,1)}, bf16[512,512]{1,0:T(8,128)(2,1)}, u32[]{:S(2)}, u32[]{:S(2)}) collective-permute-start(bf16[512,512]{1,0:T(8,128)(2,1)} %get-tuple-element.103), channel_id=1, source_target_pairs={{0,1},{1,0},{2,3},{3,2},{4,5},{5,4},{6,7},{7,6},{8,9},{9,8},{10,11... | collective-permute-start | bytes 1572872 | tf_op jit(solution)/shard_map/ppermute | solution.py:28
  61.2 4.6 %collective-permute-start.16 = (bf16[512,512]{1,0:T(8,128)(2,1)}, bf16[512,512]{1,0:T(8,128)(2,1)}, u32[]{:S(2)}, u32[]{:S(2)}) collective-permute-start(bf16[512,512]{1,0:T(8,128)(2,1)} %get-tuple-element.104), channel_id=1, source_target_pairs={{0,1},{1,0},{2,3},{3,2},{4,5},{5,4},{6,7},{7,6},{8,9},{9,8},{10,11... | collective-permute-start | bytes 1572872 | tf_op jit(solution)/shard_map/ppermute | solution.py:28
  63.3 4.7 %copy-start.1 = (bf16[256,8192]{1,0:T(8,128)(2,1)S(1)}, bf16[256,8192]{1,0:T(8,128)(2,1)}, u32[]{:S(2)}) copy-start(bf16[256,8192]{1,0:T(8,128)(2,1)} %refs_7_) | copy-start | bytes 12582916
  65.9 12.6 %collective-permute-start.20 = (s32[256,128]{1,0:T(8,128)S(1)}, s32[256,128]{1,0:T(8,128)S(1)}, u32[]{:S(2)}, u32[]{:S(2)}) collective-permute-start(s32[256,128]{1,0:T(8,128)S(1)} %add_select_fusion.1), channel_id=1, source_target_pairs={{0,64},{1,65},{2,66},{3,67},{4,68},{5,69},{6,70},{7,71},{8,72},{9,... | collective-permute-start | bytes 393224 | tf_op jit(solution)/shard_map/ppermute | solution.py:28
  67.4 26.5 %collective-permute-start.22 = (bf16[512,512]{1,0:T(8,128)(2,1)}, bf16[512,512]{1,0:T(8,128)(2,1)S(1)}, u32[]{:S(2)}, u32[]{:S(2)}) collective-permute-start(bf16[512,512]{1,0:T(8,128)(2,1)} %copy-done.9), channel_id=1, source_target_pairs={{0,2},{1,3},{2,0},{3,1},{4,6},{5,7},{6,4},{7,5},{8,10},{9,11},{10,... | collective-permute-start | bytes 1572872 | tf_op jit(solution)/shard_map/ppermute | solution.py:28
  68.0 1.6 %copy-start.5 = (bf16[1,2048,512]{2,1,0:T(8,128)(2,1)S(1)}, bf16[1,2048,512]{2,1,0:T(8,128)(2,1)}, u32[]{:S(2)}) copy-start(bf16[1,2048,512]{2,1,0:T(8,128)(2,1)} %param.13) | copy-start | bytes 6291460
  78.4 9.1 %copy-start.10 = (f32[1536,128]{1,0:T(8,128)S(1)}, f32[1536,128]{1,0:T(8,128)}, u32[]{:S(2)}) copy-start(f32[1536,128]{1,0:T(8,128)} %param.15) | copy-start | bytes 2359300
  78.5 9.1 %copy-start.11 = (f32[1536,128]{1,0:T(8,128)S(1)}, f32[1536,128]{1,0:T(8,128)}, u32[]{:S(2)}) copy-start(f32[1536,128]{1,0:T(8,128)} %param.17) | copy-start | bytes 2359300
  (4 other events, 5.1 us)
